TPU v7x, 256 devices: a whole 4x4x8 slice. The times are simulated.
256 devices in a mesh: row: 16 (over x, z_lo), col: 16 (over z_hi, y, core).
Axes of the slice: x: 4, y: 4, z: 8 (z_hi: 2, z_lo: 4; z = z_hi * 4 + z_lo), core: 2. Of those that a mesh axis runs over, the one named last changes fastest.
Arguments:
- kernel_tiles: bfloat16 [16, 16, 128, 128, 128], P('row', 'col'), may hold values from -0.046875 to 0.046875
- tile_rows: int32 [16, 16, 128], P('row', 'col'), may hold values from 0 to 31
- tile_cols: int32 [16, 16, 128], P('row', 'col'), may hold values from 0 to 31, as said below
- tile_counts: int32 [16, 16], P('row', 'col'), may hold values from 32 to 128, as said below
- noise: float32 [65536], P(('row', 'col')), may hold values from 0.1 to 1
- prev_block: float32 [32, 65536], P(None, ('row', 'col')), may hold values from -6 to 6
- current_block: float32 [32, 65536], P(None, ('row', 'col')), may hold values from -6 to 6
- prev_coupling: float32 [32, 32], replicated, may hold values from -1 to 1
Outputs:
- next_block: float32 [32, 65536], P(None, ('row', 'col'))
- diag_blocks: float32 [6, 32, 32], replicated
- coupling_blocks: float32 [6, 32, 32], replicated
Inputs may be any that keep to these rules, and one draw needn't show every extreme that they name: Entries of tile_counts lie from 32 to 128; some device is full. For the device at grid place (r, c), every tile_cols[r, c, s] // 2 lies from r - 1 to r + 1 (a band around the device's own block rows).
All inputs are finite; a program needn't handle non-finite values.
Results may differ from a plain program's by a relative error of at most 0.04.
Values may be sent and summed in bfloat16 or wider, within the bound.
A program may use at most 64 MiB of HBM per device.

v0:
```python
import jax
import jax.numpy as jnp
from jax import lax
from jax.sharding import PartitionSpec as P

ITERS = 6


def with_halo(cells, sides, width):
    for axis, dim in sides:
        count = lax.axis_size(axis)
        ends = count - 1
        head = lax.slice_in_dim(cells, 0, width, axis=dim)
        tail = lax.slice_in_dim(cells, cells.shape[dim] - width, cells.shape[dim], axis=dim)
        cells = jnp.concatenate(
            [
                lax.ppermute(tail, axis, [(i, (i + 1) % count) for i in range(ends)]),
                cells,
                lax.ppermute(head, axis, [((i + 1) % count, i) for i in range(ends)]),
            ],
            axis=dim,
        )
    return cells


def from_behind(value, axis, by):
    count = lax.axis_size(axis)
    pairs = [(i, i + by) for i in range(count) if 0 <= i + by < count]
    return lax.ppermute(value, axis, pairs)


def hdot(left, right):
    return jnp.dot(left, right, precision=lax.Precision.HIGHEST, preferred_element_type=jnp.float32)


def apply_operator(current, tiles, rows, cols, count, noise):
    vectors = current.shape[0]
    width = current.shape[1]
    side = tiles.shape[1]
    per_dev = width // side
    n_col = lax.axis_size("col")
    slot_count = tiles.shape[0]
    place = lax.axis_index("row")
    rounded = current.astype(jnp.bfloat16)
    live = (jnp.arange(slot_count, dtype=jnp.int32) < count).astype(jnp.float32)
    band_cols = cols - (place - 1) * per_dev
    row_hits = (rows[None, :] == jnp.arange(n_col * per_dev, dtype=jnp.int32)[:, None]).astype(
        jnp.float32
    ) * live[None, :]
    col_hits = (band_cols[None, :] == jnp.arange(3 * per_dev, dtype=jnp.int32)[:, None]).astype(
        jnp.float32
    ) * live[None, :]
    band_panel = with_halo(rounded, (("row", 1),), width).reshape(vectors, 3 * per_dev, side)
    picked = jnp.take(band_panel, band_cols, axis=1)
    forward = jnp.einsum("tab,ktb->kta", tiles, picked, preferred_element_type=jnp.float32)
    row_part = jnp.einsum("rt,kta->kra", row_hits, forward, precision=lax.Precision.HIGHEST)
    row_part = row_part.reshape(vectors, n_col * width)
    row_total = lax.psum_scatter(
        row_part.astype(jnp.bfloat16), "col", scatter_dimension=1, tiled=True
    ).astype(jnp.float32)
    row_panel = lax.all_gather(rounded, "col", axis=1, tiled=True).reshape(
        vectors, n_col * per_dev, side
    )
    picked_rows = jnp.take(row_panel, rows, axis=1)
    mirror = jnp.einsum("tab,kta->ktb", tiles, picked_rows, preferred_element_type=jnp.float32)
    col_part = jnp.einsum("ct,ktb->kcb", col_hits, mirror, precision=lax.Precision.HIGHEST)
    groups = col_part.reshape(vectors, 3, width)
    from_below = from_behind(groups[:, 2].astype(jnp.bfloat16), "row", 1).astype(jnp.float32)
    from_above = from_behind(groups[:, 0].astype(jnp.bfloat16), "row", -1).astype(jnp.float32)
    col_total = groups[:, 1] + from_below + from_above
    return row_total + col_total + noise[None, :] * current


def on_device(
    kernel_tiles, tile_rows, tile_cols, tile_counts, noise, prev_block, current_block, prev_coupling
):
    tiles = kernel_tiles[0, 0]
    rows = tile_rows[0, 0]
    cols = tile_cols[0, 0]
    count = tile_counts[0, 0]
    total_points = current_block.shape[1] * lax.axis_size("row") * lax.axis_size("col")
    previous = prev_block
    current = current_block
    coupling = prev_coupling
    diag_list = []
    lower_list = []
    for step in range(ITERS):
        image = apply_operator(current, tiles, rows, cols, count, noise)
        first = image - hdot(coupling, previous)
        diag = lax.psum(hdot(current, first.T), ("row", "col")) / total_points
        second = first - hdot(diag.T, current)
        back = lax.psum(hdot(previous, second.T), ("row", "col")) / total_points
        third = second - hdot(back.T, previous)
        gram = lax.psum(hdot(third, third.T), ("row", "col")) / total_points
        lower = jnp.linalg.cholesky(gram)
        following = lax.linalg.triangular_solve(lower, third, left_side=True, lower=True)
        diag_list.append(diag)
        lower_list.append(lower)
        previous = current
        current = following
        coupling = lower.T
    return (current, jnp.stack(diag_list), jnp.stack(lower_list))


def solution(mesh):
    in_specs = (
        P("row", "col", None, None, None),
        P("row", "col", None),
        P("row", "col", None),
        P("row", "col"),
        P(("row", "col")),
        P(None, ("row", "col")),
        P(None, ("row", "col")),
        P(),
    )
    out_specs = (P(None, ("row", "col")), P(), P())
    return jax.shard_map(
        on_device, mesh=mesh, in_specs=in_specs, out_specs=out_specs, check_vma=False
    )
```

profile of v0, /device:TPU:1, one launch (start us, length us, event | category | flops | bytes accessed | tf_op | source)
XLA Modules:
  0.0 2189.4 jit_solution(9503854728115010900)
XLA Ops:
  8.0 4.4 collective-permute-start
  13.7 34.0 %all_gather.18 = bf16[32,4096]{1,0:T(8,128)(2,1)S(1)} all-gather(bf16[32,256]{1,0:T(8,128)(2,1)S(1)} %convert_element_type.198), channel_id=1, replica_groups=mesh['row'=16,'col'=16] {'col'}, dimensions={1}, use_global_device_ids=true | all-gather | bytes 278528 | tf_op jit(solution)/shard_map/all_gather | solution.py:61
  57.9 4.5 fusion.48
  65.7 4.3 collective-permute-start.2
  74.5 62.5 %reduce-scatter.7.cloned.1.call-done = bf16[32,256]{1,0:T(8,128)(2,1)} async-done(((bf16[32,4096]{1,0:T(8,128)(2,1)}), bf16[32,256]{1,0:T(8,128)(2,1)}) %reduce-scatter.7.cloned.1.call-update) | async-done | bytes 16400 | tf_op jit(solution)/shard_map/reduce_scatter | solution.py:58
  137.8 75.8 %psum.126 = f32[32,32]{0,1:T(8,128)S(1)} all-reduce(f32[32,32]{0,1:T(8,128)S(1)} %convolution_bitcast_fusion.2), channel_id=1, replica_groups=mesh['row'=16,'col'=16] {'row','col'}, use_global_device_ids=true, to_apply=%region_1.0 | all-reduce | flops 1024 | bytes 8192 | tf_op jit(solution)/shard_map/psum | solution.py:90
  214.7 73.8 %psum.127 = f32[32,32]{0,1:T(8,128)S(1)} all-reduce(f32[32,32]{0,1:T(8,128)S(1)} %convolution_bitcast_fusion.1), channel_id=1, replica_groups=mesh['row'=16,'col'=16] {'row','col'}, use_global_device_ids=true, to_apply=%region_2.0 | all-reduce | flops 1024 | bytes 8192 | tf_op jit(solution)/shard_map/psum | solution.py:92
  288.8 73.7 %psum.128 = f32[32,32]{0,1:T(8,128)S(1)} all-reduce(f32[32,32]{0,1:T(8,128)S(1)} %fusion.420), channel_id=1, replica_groups=mesh['row'=16,'col'=16] {'row','col'}, use_global_device_ids=true, to_apply=%region_3.6 | all-reduce | flops 1024 | bytes 8192 | tf_op jit(solution)/shard_map/psum | solution.py:94
  369.6 3.6 collective-permute-start.4
  374.5 29.5 %all_gather.19 = bf16[32,4096]{1,0:T(8,128)(2,1)S(1)} all-gather(bf16[32,256]{1,0:T(8,128)(2,1)S(1)} %get-tuple-element.42), channel_id=1, replica_groups=mesh['row'=16,'col'=16] {'col'}, dimensions={1}, use_global_device_ids=true | all-gather | bytes 278528 | tf_op jit(solution)/shard_map/all_gather | solution.py:61
  410.7 4.3 collective-permute-start.6
  417.1 4.5 fusion.54
  425.6 73.3 %reduce-scatter.9.cloned.1.call-done = bf16[32,256]{1,0:T(8,128)(2,1)} async-done(((bf16[32,4096]{1,0:T(8,128)(2,1)}), bf16[32,256]{1,0:T(8,128)(2,1)}) %reduce-scatter.9.cloned.1.call-update) | async-done | bytes 16400 | tf_op jit(solution)/shard_map/reduce_scatter | solution.py:58
  500.6 75.8 %psum.129 = f32[32,32]{0,1:T(8,128)S(1)} all-reduce(f32[32,32]{0,1:T(8,128)S(1)} %fusion.421), channel_id=1, replica_groups=mesh['row'=16,'col'=16] {'row','col'}, use_global_device_ids=true, to_apply=%region_7.0 | all-reduce | flops 1024 | bytes 8192 | tf_op jit(solution)/shard_map/psum | solution.py:90
  576.7 74.0 %psum.130 = f32[32,32]{0,1:T(8,128)S(1)} all-reduce(f32[32,32]{0,1:T(8,128)S(1)} %convolution_bitcast_fusion), channel_id=1, replica_groups=mesh['row'=16,'col'=16] {'row','col'}, use_global_device_ids=true, to_apply=%region_8.0 | all-reduce | flops 1024 | bytes 8192 | tf_op jit(solution)/shard_map/psum | solution.py:92
  651.1 73.5 %psum.131 = f32[32,32]{0,1:T(8,128)S(1)} all-reduce(f32[32,32]{0,1:T(8,128)S(1)} %fusion.422), channel_id=1, replica_groups=mesh['row'=16,'col'=16] {'row','col'}, use_global_device_ids=true, to_apply=%region_9.0 | all-reduce | flops 1024 | bytes 8192 | tf_op jit(solution)/shard_map/psum | solution.py:94
  731.7 3.6 collective-permute-start.8
  736.6 29.5 %all_gather.20 = bf16[32,4096]{1,0:T(8,128)(2,1)S(1)} all-gather(bf16[32,256]{1,0:T(8,128)(2,1)S(1)} %get-tuple-element.44), channel_id=1, replica_groups=mesh['row'=16,'col'=16] {'col'}, dimensions={1}, use_global_device_ids=true | all-gather | bytes 278528 | tf_op jit(solution)/shard_map/all_gather | solution.py:61
  772.8 4.4 collective-permute-start.10
  779.3 4.5 fusion.60
  787.8 73.2 %reduce-scatter.11.cloned.1.call-done = bf16[32,256]{1,0:T(8,128)(2,1)} async-done(((bf16[32,4096]{1,0:T(8,128)(2,1)}), bf16[32,256]{1,0:T(8,128)(2,1)}) %reduce-scatter.11.cloned.1.call-update) | async-done | bytes 16400 | tf_op jit(solution)/shard_map/reduce_scatter | solution.py:58
  862.7 76.2 %psum.132 = f32[32,32]{0,1:T(8,128)S(1)} all-reduce(f32[32,32]{0,1:T(8,128)S(1)} %fusion.423), channel_id=1, replica_groups=mesh['row'=16,'col'=16] {'row','col'}, use_global_device_ids=true, to_apply=%region_11.0 | all-reduce | flops 1024 | bytes 8192 | tf_op jit(solution)/shard_map/psum | solution.py:90
  939.2 73.8 %psum.133 = f32[32,32]{0,1:T(8,128)S(1)} all-reduce(f32[32,32]{0,1:T(8,128)S(1)} %fusion.424), channel_id=1, replica_groups=mesh['row'=16,'col'=16] {'row','col'}, use_global_device_ids=true, to_apply=%region_12.0 | all-reduce | flops 1024 | bytes 8192 | tf_op jit(solution)/shard_map/psum | solution.py:92
  1013.4 73.5 %psum.134 = f32[32,32]{0,1:T(8,128)S(1)} all-reduce(f32[32,32]{0,1:T(8,128)S(1)} %fusion.425), channel_id=1, replica_groups=mesh['row'=16,'col'=16] {'row','col'}, use_global_device_ids=true, to_apply=%region_13.0 | all-reduce | flops 1024 | bytes 8192 | tf_op jit(solution)/shard_map/psum | solution.py:94
  1093.9 3.6 collective-permute-start.12
  1098.9 29.5 %all_gather.21 = bf16[32,4096]{1,0:T(8,128)(2,1)S(1)} all-gather(bf16[32,256]{1,0:T(8,128)(2,1)S(1)} %get-tuple-element.46), channel_id=1, replica_groups=mesh['row'=16,'col'=16] {'col'}, dimensions={1}, use_global_device_ids=true | all-gather | bytes 278528 | tf_op jit(solution)/shard_map/all_gather | solution.py:61
  1135.1 4.4 collective-permute-start.14
  1141.6 4.5 fusion.66
  1150.2 73.0 %reduce-scatter.13.cloned.1.call-done = bf16[32,256]{1,0:T(8,128)(2,1)} async-done(((bf16[32,4096]{1,0:T(8,128)(2,1)}), bf16[32,256]{1,0:T(8,128)(2,1)}) %reduce-scatter.13.cloned.1.call-update) | async-done | bytes 16400 | tf_op jit(solution)/shard_map/reduce_scatter | solution.py:58
  1225.0 75.8 %psum.135 = f32[32,32]{0,1:T(8,128)S(1)} all-reduce(f32[32,32]{0,1:T(8,128)S(1)} %fusion.426), channel_id=1, replica_groups=mesh['row'=16,'col'=16] {'row','col'}, use_global_device_ids=true, to_apply=%region_15.0 | all-reduce | flops 1024 | bytes 8192 | tf_op jit(solution)/shard_map/psum | solution.py:90
  1301.1 73.8 %psum.136 = f32[32,32]{0,1:T(8,128)S(1)} all-reduce(f32[32,32]{0,1:T(8,128)S(1)} %fusion.427), channel_id=1, replica_groups=mesh['row'=16,'col'=16] {'row','col'}, use_global_device_ids=true, to_apply=%region_16.0 | all-reduce | flops 1024 | bytes 8192 | tf_op jit(solution)/shard_map/psum | solution.py:92
  1375.3 73.5 %psum.137 = f32[32,32]{0,1:T(8,128)S(1)} all-reduce(f32[32,32]{0,1:T(8,128)S(1)} %fusion.428), channel_id=1, replica_groups=mesh['row'=16,'col'=16] {'row','col'}, use_global_device_ids=true, to_apply=%region_17.0 | all-reduce | flops 1024 | bytes 8192 | tf_op jit(solution)/shard_map/psum | solution.py:94
  1455.9 3.6 collective-permute-start.16
  1460.8 29.4 %all_gather.22 = bf16[32,4096]{1,0:T(8,128)(2,1)S(1)} all-gather(bf16[32,256]{1,0:T(8,128)(2,1)S(1)} %get-tuple-element.48), channel_id=1, replica_groups=mesh['row'=16,'col'=16] {'col'}, dimensions={1}, use_global_device_ids=true | all-gather | bytes 278528 | tf_op jit(solution)/shard_map/all_gather | solution.py:61
  1496.9 4.3 collective-permute-start.18
  1503.5 4.5 fusion.72
  1512.0 73.3 %reduce-scatter.15.cloned.1.call-done = bf16[32,256]{1,0:T(8,128)(2,1)} async-done(((bf16[32,4096]{1,0:T(8,128)(2,1)}), bf16[32,256]{1,0:T(8,128)(2,1)}) %reduce-scatter.15.cloned.1.call-update) | async-done | bytes 16400 | tf_op jit(solution)/shard_map/reduce_scatter | solution.py:58
  1587.1 75.7 %psum.138 = f32[32,32]{0,1:T(8,128)S(1)} all-reduce(f32[32,32]{0,1:T(8,128)S(1)} %fusion.429), channel_id=1, replica_groups=mesh['row'=16,'col'=16] {'row','col'}, use_global_device_ids=true, to_apply=%region_19.0 | all-reduce | flops 1024 | bytes 8192 | tf_op jit(solution)/shard_map/psum | solution.py:90
  1663.1 74.0 %psum.139 = f32[32,32]{0,1:T(8,128)S(1)} all-reduce(f32[32,32]{0,1:T(8,128)S(1)} %fusion.430), channel_id=1, replica_groups=mesh['row'=16,'col'=16] {'row','col'}, use_global_device_ids=true, to_apply=%region_20.0 | all-reduce | flops 1024 | bytes 8192 | tf_op jit(solution)/shard_map/psum | solution.py:92
  1737.5 73.5 %psum.140 = f32[32,32]{0,1:T(8,128)S(1)} all-reduce(f32[32,32]{0,1:T(8,128)S(1)} %fusion.431), channel_id=1, replica_groups=mesh['row'=16,'col'=16] {'row','col'}, use_global_device_ids=true, to_apply=%region_21.0 | all-reduce | flops 1024 | bytes 8192 | tf_op jit(solution)/shard_map/psum | solution.py:94
  1818.1 3.6 collective-permute-start.20
  1823.0 29.6 %all_gather.23 = bf16[32,4096]{1,0:T(8,128)(2,1)S(1)} all-gather(bf16[32,256]{1,0:T(8,128)(2,1)S(1)} %get-tuple-element.50), channel_id=1, replica_groups=mesh['row'=16,'col'=16] {'col'}, dimensions={1}, use_global_device_ids=true | all-gather | bytes 278528 | tf_op jit(solution)/shard_map/all_gather | solution.py:61
  1859.3 4.3 collective-permute-start.22
  1865.7 4.5 fusion.78
  1874.1 73.3 %reduce-scatter.17.cloned.1.call-done = bf16[32,256]{1,0:T(8,128)(2,1)} async-done(((bf16[32,4096]{1,0:T(8,128)(2,1)}), bf16[32,256]{1,0:T(8,128)(2,1)}) %reduce-scatter.17.cloned.1.call-update) | async-done | bytes 16400 | tf_op jit(solution)/shard_map/reduce_scatter | solution.py:58
  1949.2 75.8 %psum.141 = f32[32,32]{0,1:T(8,128)S(1)} all-reduce(f32[32,32]{0,1:T(8,128)S(1)} %fusion.432), channel_id=1, replica_groups=mesh['row'=16,'col'=16] {'row','col'}, use_global_device_ids=true, to_apply=%region_23.0 | all-reduce | flops 1024 | bytes 8192 | tf_op jit(solution)/shard_map/psum | solution.py:90
  2025.4 73.8 %psum.142 = f32[32,32]{0,1:T(8,128)S(1)} all-reduce(f32[32,32]{0,1:T(8,128)S(1)} %fusion.433), channel_id=1, replica_groups=mesh['row'=16,'col'=16] {'row','col'}, use_global_device_ids=true, to_apply=%region_24.0 | all-reduce | flops 1024 | bytes 8192 | tf_op jit(solution)/shard_map/psum | solution.py:92
  2099.5 73.5 %psum.143 = f32[32,32]{0,1:T(8,128)S(1)} all-reduce(f32[32,32]{0,1:T(8,128)S(1)} %fusion.434), channel_id=1, replica_groups=mesh['row'=16,'col'=16] {'row','col'}, use_global_device_ids=true, to_apply=%region_25.0 | all-reduce | flops 1024 | bytes 8192 | tf_op jit(solution)/shard_map/psum | solution.py:94
  (237 shorter events, 147.9 us)
Async XLA Ops:
  7.2 64.1 %copy-start = (f32[32,256]{1,0:T(8,128)S(1)}, f32[32,256]{1,0:T(8,128)}, u32[]{:S(2)}) copy-start(f32[32,256]{1,0:T(8,128)} %param.20) | copy-start | bytes 98308
  7.2 129.7 %reduce-scatter.7.cloned.1.call-start = ((), (), s32[]{:S(2)}) async-start(), calls=%async_computation.6 | async-start | bytes 278528 | tf_op jit(solution)/shard_map/reduce_scatter | solution.py:58
  8.0 49.1 %collective-permute-start = (bf16[32,256]{1,0:T(8,128)(2,1)S(1)}, bf16[32,256]{1,0:T(8,128)(2,1)S(1)}, u32[]{:S(2)}, u32[]{:S(2)}) collective-permute-start(bf16[32,256]{1,0:T(8,128)(2,1)S(1)} %convert_element_type.198), channel_id=1, source_target_pairs={{0,16},{16,32},{32,48},{48,64},{64,80},{80,96},{96,112},{112,128},... | collective-permute-start | bytes 49160 | tf_op jit(solution)/shard_map/ppermute | solution.py:17
  12.4 44.7 %collective-permute-start.1 = (bf16[32,256]{1,0:T(8,128)(2,1)S(1)}, bf16[32,256]{1,0:T(8,128)(2,1)S(1)}, u32[]{:S(2)}, u32[]{:S(2)}) collective-permute-start(bf16[32,256]{1,0:T(8,128)(2,1)S(1)} %convert_element_type.198), channel_id=1, source_target_pairs={{16,0},{32,16},{48,32},{64,48},{80,64},{96,80},{112,96},{128,112},... | collective-permute-start | bytes 49160 | tf_op jit(solution)/shard_map/ppermute | solution.py:19
  57.8 4.6 copy-start.3
  62.4 8.9 copy-start.4
  62.4 74.5 %copy-start.1 = (f32[32,256]{1,0:T(8,128)S(1)}, f32[32,256]{1,0:T(8,128)}, u32[]{:S(2)}) copy-start(f32[32,256]{1,0:T(8,128)} %param.21) | copy-start | bytes 98308
  62.4 74.5 %copy-start.2 = (f32[256]{0:T(256)S(1)}, f32[256]{0:T(256)}, u32[]{:S(2)}) copy-start(f32[256]{0:T(256)} %param.19) | copy-start | bytes 3076
  65.6 433.2 %reduce-scatter.9.cloned.1.call-start = ((), (), s32[]{:S(2)}) async-start(), calls=%async_computation.7 | async-start | bytes 278528 | tf_op jit(solution)/shard_map/reduce_scatter | solution.py:58
  65.7 5.8 collective-permute-start.2
  70.0 4.5 collective-permute-start.3
  369.6 46.7 %collective-permute-start.4 = (bf16[32,256]{1,0:T(8,128)(2,1)S(1)}, bf16[32,256]{1,0:T(8,128)(2,1)S(1)}, u32[]{:S(2)}, u32[]{:S(2)}) collective-permute-start(bf16[32,256]{1,0:T(8,128)(2,1)S(1)} %get-tuple-element.42), channel_id=1, source_target_pairs={{0,16},{16,32},{32,48},{48,64},{64,80},{80,96},{96,112},{112,128},... | collective-permute-start | bytes 49160 | tf_op jit(solution)/shard_map/ppermute | solution.py:17
  373.2 43.1 %collective-permute-start.5 = (bf16[32,256]{1,0:T(8,128)(2,1)S(1)}, bf16[32,256]{1,0:T(8,128)(2,1)S(1)}, u32[]{:S(2)}, u32[]{:S(2)}) collective-permute-start(bf16[32,256]{1,0:T(8,128)(2,1)S(1)} %get-tuple-element.42), channel_id=1, source_target_pairs={{16,0},{32,16},{48,32},{64,48},{80,64},{96,80},{112,96},{128,112},... | collective-permute-start | bytes 49160 | tf_op jit(solution)/shard_map/ppermute | solution.py:19
  410.7 14.9 collective-permute-start.6
  415.0 10.6 collective-permute-start.7
  424.8 436.1 %reduce-scatter.11.cloned.1.call-start = ((), (), s32[]{:S(2)}) async-start(), calls=%async_computation.8 | async-start | bytes 278528 | tf_op jit(solution)/shard_map/reduce_scatter | solution.py:58
  731.7 46.8 %collective-permute-start.8 = (bf16[32,256]{1,0:T(8,128)(2,1)S(1)}, bf16[32,256]{1,0:T(8,128)(2,1)S(1)}, u32[]{:S(2)}, u32[]{:S(2)}) collective-permute-start(bf16[32,256]{1,0:T(8,128)(2,1)S(1)} %get-tuple-element.44), channel_id=1, source_target_pairs={{0,16},{16,32},{32,48},{48,64},{64,80},{80,96},{96,112},{112,128},... | collective-permute-start | bytes 49160 | tf_op jit(solution)/shard_map/ppermute | solution.py:17
  735.3 43.2 %collective-permute-start.9 = (bf16[32,256]{1,0:T(8,128)(2,1)S(1)}, bf16[32,256]{1,0:T(8,128)(2,1)S(1)}, u32[]{:S(2)}, u32[]{:S(2)}) collective-permute-start(bf16[32,256]{1,0:T(8,128)(2,1)S(1)} %get-tuple-element.44), channel_id=1, source_target_pairs={{16,0},{32,16},{48,32},{64,48},{80,64},{96,80},{112,96},{128,112},... | collective-permute-start | bytes 49160 | tf_op jit(solution)/shard_map/ppermute | solution.py:19
  772.8 15.0 collective-permute-start.10
  777.2 10.6 collective-permute-start.11
  787.0 436.2 %reduce-scatter.13.cloned.1.call-start = ((), (), s32[]{:S(2)}) async-start(), calls=%async_computation.9 | async-start | bytes 278528 | tf_op jit(solution)/shard_map/reduce_scatter | solution.py:58
  1093.9 46.8 %collective-permute-start.12 = (bf16[32,256]{1,0:T(8,128)(2,1)S(1)}, bf16[32,256]{1,0:T(8,128)(2,1)S(1)}, u32[]{:S(2)}, u32[]{:S(2)}) collective-permute-start(bf16[32,256]{1,0:T(8,128)(2,1)S(1)} %get-tuple-element.46), channel_id=1, source_target_pairs={{0,16},{16,32},{32,48},{48,64},{64,80},{80,96},{96,112},{112,128},... | collective-permute-start | bytes 49160 | tf_op jit(solution)/shard_map/ppermute | solution.py:17
  1097.6 43.2 %collective-permute-start.13 = (bf16[32,256]{1,0:T(8,128)(2,1)S(1)}, bf16[32,256]{1,0:T(8,128)(2,1)S(1)}, u32[]{:S(2)}, u32[]{:S(2)}) collective-permute-start(bf16[32,256]{1,0:T(8,128)(2,1)S(1)} %get-tuple-element.46), channel_id=1, source_target_pairs={{16,0},{32,16},{48,32},{64,48},{80,64},{96,80},{112,96},{128,112},... | collective-permute-start | bytes 49160 | tf_op jit(solution)/shard_map/ppermute | solution.py:19
  1135.1 15.1 collective-permute-start.14
  1139.4 10.8 collective-permute-start.15
  1149.3 436.0 %reduce-scatter.15.cloned.1.call-start = ((), (), s32[]{:S(2)}) async-start(), calls=%async_computation.10 | async-start | bytes 278528 | tf_op jit(solution)/shard_map/reduce_scatter | solution.py:58
  1455.9 46.9 %collective-permute-start.16 = (bf16[32,256]{1,0:T(8,128)(2,1)S(1)}, bf16[32,256]{1,0:T(8,128)(2,1)S(1)}, u32[]{:S(2)}, u32[]{:S(2)}) collective-permute-start(bf16[32,256]{1,0:T(8,128)(2,1)S(1)} %get-tuple-element.48), channel_id=1, source_target_pairs={{0,16},{16,32},{32,48},{48,64},{64,80},{80,96},{96,112},{112,128},... | collective-permute-start | bytes 49160 | tf_op jit(solution)/shard_map/ppermute | solution.py:17
  1459.5 43.3 %collective-permute-start.17 = (bf16[32,256]{1,0:T(8,128)(2,1)S(1)}, bf16[32,256]{1,0:T(8,128)(2,1)S(1)}, u32[]{:S(2)}, u32[]{:S(2)}) collective-permute-start(bf16[32,256]{1,0:T(8,128)(2,1)S(1)} %get-tuple-element.48), channel_id=1, source_target_pairs={{16,0},{32,16},{48,32},{64,48},{80,64},{96,80},{112,96},{128,112},... | collective-permute-start | bytes 49160 | tf_op jit(solution)/shard_map/ppermute | solution.py:19
  1496.9 15.1 collective-permute-start.18
  1501.2 10.8 collective-permute-start.19
  1511.3 436.2 %reduce-scatter.17.cloned.1.call-start = ((), (), s32[]{:S(2)}) async-start(), calls=%async_computation.11 | async-start | bytes 278528 | tf_op jit(solution)/shard_map/reduce_scatter | solution.py:58
  1818.1 46.8 %collective-permute-start.20 = (bf16[32,256]{1,0:T(8,128)(2,1)S(1)}, bf16[32,256]{1,0:T(8,128)(2,1)S(1)}, u32[]{:S(2)}, u32[]{:S(2)}) collective-permute-start(bf16[32,256]{1,0:T(8,128)(2,1)S(1)} %get-tuple-element.50), channel_id=1, source_target_pairs={{0,16},{16,32},{32,48},{48,64},{64,80},{80,96},{96,112},{112,128},... | collective-permute-start | bytes 49160 | tf_op jit(solution)/shard_map/ppermute | solution.py:17
  1821.7 43.2 %collective-permute-start.21 = (bf16[32,256]{1,0:T(8,128)(2,1)S(1)}, bf16[32,256]{1,0:T(8,128)(2,1)S(1)}, u32[]{:S(2)}, u32[]{:S(2)}) collective-permute-start(bf16[32,256]{1,0:T(8,128)(2,1)S(1)} %get-tuple-element.50), channel_id=1, source_target_pairs={{16,0},{32,16},{48,32},{64,48},{80,64},{96,80},{112,96},{128,112},... | collective-permute-start | bytes 49160 | tf_op jit(solution)/shard_map/ppermute | solution.py:19
  1859.3 14.8 collective-permute-start.22
  1863.6 10.6 collective-permute-start.23
  2178.1 4.1 copy-start.5
Sparse Core Ops, SparseCore 0:
  65.8 71.1 reduce-scatter.6
  424.9 73.8 reduce-scatter.8
  787.1 73.7 reduce-scatter.10
  1149.4 73.7 reduce-scatter.12
  1511.4 73.8 reduce-scatter.14
  1873.6 73.8 reduce-scatter.16
where the time goes:
time: 2200 us; the launch traced here: 2190 us
  blocking collectives  1520 us (69%)
  waiting for transfers between devices  432 us (20%)
  matrix products  92.8 us (4%)
  starting transfers between devices  64.4 us (3%)
  other arithmetic  47.1 us (2%)
    psum x6, blocking collectives, on_device(): diag = lax.psum(hdot(current, first.T), ('row', 'col')) / total_points  455 us
    psum x6, blocking collectives, on_device(): back = lax.psum(hdot(previous, second.T), ('row', 'col')) / total_points  443 us
    psum x6, blocking collectives, on_device(): gram = lax.psum(hdot(third, third.T), ('row', 'col')) / total_points  441 us
    reduce_scatter x6, waiting for transfers between devices, apply_operator(): lax.psum_scatter(row_part.astype(jnp.bfloat16), 'col', scatter_dimension=...  428 us
    all_gather x6, blocking collectives, apply_operator(): lax.all_gather(rounded, 'col', axis=1, tiled=True)  181 us
  transfers between devices with their start and end apart: 30, of which 7 were waited for; matrix products, arithmetic and copies ran while one was open for 4% of the time, Pallas kernels for 0%

commit v1 on v0

v1 whole, which is shorter than its diff:
```python
import jax
import jax.numpy as jnp
from jax import lax
from jax.experimental import pallas as pl
from jax.experimental.pallas import tpu as pltpu
from jax.sharding import PartitionSpec as P

ITERS = 6
K = 32
BS = 128
WIDTH = 256
N_ROW = 16
N_COL = 16
SLOTS = 128
PLANE = 8
MESH_IDS = pl.DeviceIdType.MESH
F32 = jnp.float32
BF16 = jnp.bfloat16


def dot_nn(left, right):
    return lax.dot_general(
        left, right, (((1,), (0,)), ((), ())), precision=lax.Precision.HIGHEST, preferred_element_type=F32
    )


def dot_nt(left, right):
    return lax.dot_general(
        left, right, (((1,), (1,)), ((), ())), precision=lax.Precision.HIGHEST, preferred_element_type=F32
    )


def band_kernel(rows_ref, cols_ref, count_ref, tiles_hbm, band_ref, tiles, total, sems):
    parts = 4
    size = SLOTS // parts
    copies = [
        pltpu.make_async_copy(
            tiles_hbm.at[pl.ds(k * size, size)], tiles.at[pl.ds(k * size, size)], sems.at[k]
        )
        for k in range(parts)
    ]
    for copy in copies:
        copy.start()

    def clear(i, carry):
        total[i] = jnp.zeros(total.shape[1:], F32)
        return carry

    lax.fori_loop(0, 2 * N_COL, clear, 0)
    first_col = 2 * (lax.axis_index("row") - 1)
    count = count_ref[0, 0]

    def add(slot, carry):
        i = rows_ref[0, slot]
        j = cols_ref[0, slot] - first_col
        total[i, j] += tiles[slot].astype(F32)
        return carry

    for k in range(parts):
        copies[k].wait()
        lax.fori_loop(k * size, jnp.minimum((k + 1) * size, count), add, 0)

    def place(c, carry):
        for half in range(2):
            for j in range(6):
                band_ref[c, half * BS : (half + 1) * BS, j * BS : (j + 1) * BS] = total[
                    2 * c + half, j
                ].astype(BF16)
        return carry

    lax.fori_loop(0, N_COL, place, 0)


def build_band(tiles, rows, cols, count):
    smem = pl.BlockSpec(memory_space=pltpu.SMEM)
    return pl.pallas_call(
        band_kernel,
        out_shape=jax.ShapeDtypeStruct((N_COL, 2 * BS, 6 * BS), BF16),
        in_specs=[smem, smem, smem, pl.BlockSpec(memory_space=pl.ANY)],
        out_specs=pl.BlockSpec(memory_space=pltpu.VMEM),
        scratch_shapes=[
            pltpu.VMEM((SLOTS, BS, BS), BF16),
            pltpu.VMEM((2 * N_COL, 6, BS, BS), F32),
            pltpu.SemaphoreType.DMA((4,)),
        ],
        compiler_params=pltpu.CompilerParams(vmem_limit_bytes=40 * 2**20),
        name="band",
    )(rows, cols, count, tiles)


def factor(gram):
    groups = K // 8
    sub = lax.broadcasted_iota(jnp.int32, (8, K), 0)
    lane = lax.broadcasted_iota(jnp.int32, (8, K), 1)
    g = [gram[8 * b : 8 * b + 8] for b in range(groups)]
    e = [jnp.where(lane == sub + 8 * b, 1.0, 0.0).astype(F32) for b in range(groups)]
    step = 4
    for base in range(0, K, step):
        a = base // 8
        spread = [
            [
                jnp.broadcast_to(g[b][:, base + j : base + j + 1], (8, K)) if b >= a else None
                for b in range(groups)
            ]
            for j in range(step)
        ]
        for j in range(step):
            s = (base + j) % 8
            pivot = spread[j][a][s : s + 1]
            guess = lax.rsqrt(pivot)
            scale = guess * (1.5 - 0.5 * (pivot * guess) * guess)
            g_row = g[a][s : s + 1] * scale
            e_row = e[a][s : s + 1] * scale
            later = {jj: spread[jj][a][s : s + 1] * scale for jj in range(j + 1, step)}
            for b in range(a, groups):
                part = spread[j][b] * scale
                if b == a:
                    part = jnp.where(sub > s, part, 0.0)
                g[b] = g[b] - part * g_row
                e[b] = e[b] - part * e_row
                for jj in range(j + 1, step):
                    spread[jj][b] = spread[jj][b] - part * later[jj]
            g[a] = jnp.where(sub == s, g_row, g[a])
            e[a] = jnp.where(sub == s, e_row, e[a])
    upper = [jnp.where(lane >= sub + 8 * b, g[b], 0.0) for b in range(groups)]
    return jnp.concatenate(upper, axis=0), jnp.concatenate(e, axis=0)


def lanczos_kernel(
    band_hbm, noise_ref, prev_ref, cur_ref, coup_ref,
    out_ref, diag_ref, upper_ref,
    band, y, coup, xband, xrows, fsend, fown, frecv, zsend, zrecv, msend, mrecv, mir,
    hloc, h1, s2, h2, h3,
    band_sem, send_sems, recv_sems, sum_send, sum_recv,
):
    r = lax.axis_index("row")
    c = lax.axis_index("col")
    x, zl = r // 4, r % 4
    zh, p = c // PLANE, c % PLANE
    z = zh * 4 + zl
    m = x * PLANE + p
    up = (lax.rem(r + 1, N_ROW), c)
    down = (lax.rem(r + N_ROW - 1, N_ROW), c)
    over = (r, lax.rem(c + PLANE, N_COL))

    def plane_dev(pp):
        return (r, zh * PLANE + pp)

    def ring_dev(zz):
        return (x * 4 + zz % 4, (zz // 4) * PLANE + p)

    def sheet_dev(mm):
        return ((mm // PLANE) * 4 + zl, zh * PLANE + mm % PLANE)

    def put(src, dst, send, recv, dev):
        pltpu.make_async_remote_copy(
            src_ref=src, dst_ref=dst, send_sem=send, recv_sem=recv, device_id=dev, device_id_type=MESH_IDS
        ).start()

    def take(ref, sem):
        pltpu.make_async_copy(ref, ref, sem).wait()

    load = pltpu.make_async_copy(band_hbm, band, band_sem)
    load.start()

    barrier = pltpu.get_barrier_semaphore()

    def greet(dev):
        pl.semaphore_signal(barrier, inc=1, device_id=dev, device_id_type=MESH_IDS)

    def greet_ring(d, carry):
        greet(ring_dev(lax.rem(z + d, PLANE)))
        return carry

    def greet_sheet(d, carry):
        greet(sheet_dev(lax.rem(m + d, 32)))
        return carry

    greet(up)
    greet(down)
    lax.fori_loop(1, PLANE, greet_ring, 0)
    lax.fori_loop(1, 32, greet_sheet, 0)
    y[K : 2 * K] = cur_ref[...]
    y[2 * K : 3 * K] = prev_ref[...]
    y[3 * K : 4 * K] = prev_ref[...]
    coup[...] = coup_ref[...]
    pl.semaphore_wait(barrier, 2 + 7 + 31)

    def forward(pp):
        out = []
        for hi in range(2):
            rows = band.at[hi * PLANE + pp]
            acc = None
            for g in range(3):
                term = lax.dot_general(
                    xband[g], rows[:, g * WIDTH : (g + 1) * WIDTH], (((1,), (1,)), ((), ())),
                    preferred_element_type=F32,
                )
                acc = term if acc is None else acc + term
            out.append(acc)
        return out

    def forward_send(d, carry):
        pp = lax.rem(p + d, PLANE)
        part = forward(pp)
        for hi in range(2):
            fsend[d - 1, hi] = part[hi].astype(BF16)
        put(fsend.at[d - 1], frecv.at[d - 1], send_sems.at[4], recv_sems.at[4], plane_dev(pp))
        return carry

    def mirror(hi, first):
        def body(k, carry):
            acc = None
            for u in range(4):
                pp = 4 * k + u
                term = jnp.dot(xrows[hi, pp], band[hi * PLANE + pp], preferred_element_type=F32)
                acc = term if acc is None else acc + term
            if first:
                mir[...] = jnp.where(k == 0, acc, mir[...] + acc)
            else:
                mir[...] += acc
            return carry

        lax.fori_loop(0, 2, body, 0)

    def iteration(it, carry):
        parity = lax.rem(it, 2)
        rounded = y[K : 2 * K].astype(BF16)
        xband[1] = rounded
        xrows[zh, p] = rounded
        own = xband.at[1]
        put(own, xband.at[0], send_sems.at[0], recv_sems.at[0], up)
        put(own, xband.at[2], send_sems.at[0], recv_sems.at[0], down)
        put(own, xrows.at[zh, p], send_sems.at[1], recv_sems.at[1], over)

        def spread_own(d, carry):
            put(own, xrows.at[zh, p], send_sems.at[2], recv_sems.at[2], plane_dev(lax.rem(p + d, PLANE)))
            return carry

        lax.fori_loop(1, PLANE, spread_own, 0)

        @pl.when(it == 0)
        def _():
            load.wait()

        take(xband.at[pl.ds(0, 2)], recv_sems.at[0])
        lax.fori_loop(1, 5, forward_send, 0)
        take(zrecv, recv_sems.at[1])
        other = xrows.at[1 - zh, p]

        def spread_other(d, carry):
            put(
                other, xrows.at[1 - zh, p], send_sems.at[3], recv_sems.at[3],
                plane_dev(lax.rem(p + d, PLANE)),
            )
            return carry

        lax.fori_loop(1, PLANE, spread_other, 0)
        lax.fori_loop(5, PLANE, forward_send, 0)
        part = forward(p)
        for hi in range(2):
            fown[hi] = part[hi]
        seven = xrows.at[0, pl.ds(0, 7)]
        take(seven, recv_sems.at[2])
        mirror(zh, True)
        take(frecv, recv_sems.at[4])

        def total(hi):
            acc = fown[hi]
            for d in range(7):
                acc = acc + frecv[d, hi].astype(F32)
            return acc

        zsend[...] = total(1 - zh).astype(BF16)
        put(zsend, zrecv, send_sems.at[5], recv_sems.at[5], over)
        fown[zh] = total(zh)
        take(seven, recv_sems.at[3])
        take(seven, send_sems.at[3])
        mirror(1 - zh, False)
        msend[0] = mir[:, :WIDTH].astype(BF16)
        msend[1] = mir[:, 2 * WIDTH :].astype(BF16)
        put(msend.at[0], mrecv.at[0], send_sems.at[6], recv_sems.at[6], down)
        put(msend.at[1], mrecv.at[1], send_sems.at[6], recv_sems.at[6], up)
        base = fown[zh] + mir[:, WIDTH : 2 * WIDTH] + noise_ref[...] * y[K : 2 * K]
        take(zrecv, recv_sems.at[5])
        base = base + zrecv[...].astype(F32)
        take(mrecv, recv_sems.at[6])
        y[0:K] = base + mrecv[0].astype(F32) + mrecv[1].astype(F32)

        gram = dot_nt(y[0 : 3 * K], y[...])
        lane = lax.broadcasted_iota(jnp.int32, (K, 4 * K), 1)
        top = jnp.where(lane < 3 * K, gram[0:K], gram[2 * K : 3 * K])
        hloc[0:4] = top.reshape(4, 8, 4 * K)
        hloc[4:8] = gram[K : 2 * K].reshape(4, 8, 4 * K)

        def send1(d, carry):
            zz = lax.rem(z + d, PLANE)
            put(hloc.at[zz], h1.at[z], sum_send.at[0], sum_recv.at[0], ring_dev(zz))
            return carry

        lax.fori_loop(1, PLANE, send1, 0)
        h1[z] = hloc[z]
        take(h1.at[pl.ds(0, 7)], sum_recv.at[0])
        piece = jnp.sum(h1[...], axis=0)
        s2[...] = piece
        h2[parity, m] = piece

        def send2(d, carry):
            put(
                s2, h2.at[parity, m], sum_send.at[1], sum_recv.at[1 + parity],
                sheet_dev(lax.rem(m + d, 32)),
            )
            return carry

        lax.fori_loop(1, 32, send2, 0)
        take(h2.at[parity, pl.ds(0, 31)], sum_recv.at[1 + parity])
        h3[z] = jnp.sum(h2[parity], axis=0)

        def send3(d, carry):
            put(h3.at[z], h3.at[z], sum_send.at[2], sum_recv.at[3], ring_dev(lax.rem(z + d, PLANE)))
            return carry

        lax.fori_loop(1, PLANE, send3, 0)
        take(h1.at[pl.ds(0, 7)], sum_recv.at[3])
        h = h3[...].reshape(8 * PLANE, 4 * K) * (1.0 / (N_ROW * N_COL * WIDTH))

        im_im, im_q, im_p, p_p = (h[0:K, k * K : (k + 1) * K] for k in range(4))
        q_im, q_q, q_p = (h[K : 2 * K, k * K : (k + 1) * K] for k in range(3))
        b = coup[...]
        diag_t = im_q - dot_nt(b, q_p)
        back_t = im_p - dot_nn(b, p_p) - dot_nn(diag_t, q_p)
        cp = b + back_t
        third = y[0:K] - dot_nn(cp, y[2 * K : 3 * K]) - dot_nn(diag_t, y[K : 2 * K])
        t_im = im_im - dot_nn(diag_t, q_im) - dot_nt(cp, im_p)
        t_q = im_q - dot_nn(diag_t, q_q) - dot_nt(cp, q_p)
        t_p = im_p - dot_nn(diag_t, q_p) - dot_nn(cp, p_p)
        upper, inverse = factor(t_im - dot_nt(t_q, diag_t) - dot_nt(t_p, cp))
        diag_ref[it] = diag_t
        upper_ref[it] = upper
        coup[...] = upper
        old = y[K : 2 * K]
        y[2 * K : 3 * K] = old
        y[3 * K : 4 * K] = old
        y[K : 2 * K] = dot_nn(inverse, third)

        take(xband.at[pl.ds(0, 2)], send_sems.at[0])
        take(zsend, send_sems.at[1])
        take(seven, send_sems.at[2])
        take(frecv, send_sems.at[4])
        take(zsend, send_sems.at[5])
        take(msend, send_sems.at[6])
        take(h1.at[pl.ds(0, 7)], sum_send.at[0])
        take(h2.at[parity, pl.ds(0, 31)], sum_send.at[1])
        take(h1.at[pl.ds(0, 7)], sum_send.at[2])
        return carry

    lax.fori_loop(0, ITERS, iteration, 0)
    out_ref[...] = y[K : 2 * K]


def lanczos(band, noise, previous, current, coupling):
    vmem = pl.BlockSpec(memory_space=pltpu.VMEM)
    panel = (K, WIDTH)
    return pl.pallas_call(
        lanczos_kernel,
        out_shape=(
            jax.ShapeDtypeStruct(panel, F32),
            jax.ShapeDtypeStruct((ITERS, K, K), F32),
            jax.ShapeDtypeStruct((ITERS, K, K), F32),
        ),
        in_specs=[pl.BlockSpec(memory_space=pl.ANY), vmem, vmem, vmem, vmem],
        out_specs=(vmem, vmem, vmem),
        scratch_shapes=[
            pltpu.VMEM((N_COL, 2 * BS, 6 * BS), BF16),
            pltpu.VMEM((4 * K, WIDTH), F32),
            pltpu.VMEM((K, K), F32),
            pltpu.VMEM((3,) + panel, BF16),
            pltpu.VMEM((2, PLANE) + panel, BF16),
            pltpu.VMEM((7, 2) + panel, BF16),
            pltpu.VMEM((2,) + panel, F32),
            pltpu.VMEM((7, 2) + panel, BF16),
            pltpu.VMEM(panel, BF16),
            pltpu.VMEM(panel, BF16),
            pltpu.VMEM((2,) + panel, BF16),
            pltpu.VMEM((2,) + panel, BF16),
            pltpu.VMEM((K, 3 * WIDTH), F32),
            pltpu.VMEM((8, 8, 4 * K), F32),
            pltpu.VMEM((8, 8, 4 * K), F32),
            pltpu.VMEM((8, 4 * K), F32),
            pltpu.VMEM((2, 32, 8, 4 * K), F32),
            pltpu.VMEM((8, 8, 4 * K), F32),
            pltpu.SemaphoreType.DMA,
            pltpu.SemaphoreType.DMA((7,)),
            pltpu.SemaphoreType.DMA((7,)),
            pltpu.SemaphoreType.DMA((3,)),
            pltpu.SemaphoreType.DMA((4,)),
        ],
        compiler_params=pltpu.CompilerParams(
            collective_id=0, has_side_effects=True, vmem_limit_bytes=40 * 2**20
        ),
        name="lanczos",
    )(band, noise, previous, current, coupling)


def on_device(
    kernel_tiles, tile_rows, tile_cols, tile_counts, noise, prev_block, current_block, prev_coupling
):
    band = build_band(kernel_tiles[0, 0], tile_rows[0], tile_cols[0], tile_counts)
    following, diag_t, upper = lanczos(band, noise[None, :], prev_block, current_block, prev_coupling)
    return (following, jnp.swapaxes(diag_t, 1, 2), jnp.swapaxes(upper, 1, 2))


def solution(mesh):
    in_specs = (
        P("row", "col", None, None, None),
        P("row", "col", None),
        P("row", "col", None),
        P("row", "col"),
        P(("row", "col")),
        P(None, ("row", "col")),
        P(None, ("row", "col")),
        P(),
    )
    out_specs = (P(None, ("row", "col")), P(), P())
    return jax.shard_map(
        on_device, mesh=mesh, in_specs=in_specs, out_specs=out_specs, check_vma=False
    )
```

time: 2200 us -> 224 us (0.10)
  blocking collectives: 1520 us -> 0 us
  waiting for transfers between devices: 432 us -> 0 us
  Pallas kernels: 0 us -> 217 us
  matrix products: 92.8 us -> 0 us
  starting transfers between devices: 64.4 us -> 0 us
  other arithmetic: 47.1 us -> 0 us
    psum x18 -> x0, blocking collectives: 1340 us -> none  [the longest x6 455 us: on_device(): diag = lax.psum(hdot(current, first.T), ('row', 'col')) / total_points]
    reduce_scatter x6 -> x0, waiting for transfers between devices: 428 us -> none  [apply_operator(): lax.psum_scatter(row_part.astype(jnp.bfloat16), 'col', scatter_dimension=...]
    pallas_call x0 -> x2, Pallas kernels: none -> 217 us  [the longest x1 213 us: lanczos(): pl.pallas_call(lanczos_kernel, out_shape=(jax.ShapeDtypeStruct(panel, F32...]
    all_gather x6 -> x0, blocking collectives: 181 us -> none  [apply_operator(): lax.all_gather(rounded, 'col', axis=1, tiled=True)]
    dot_general x60 -> x0, matrix products: 90.7 us -> none  [the longest x6 27.1 us: apply_operator(): jnp.einsum('tab,ktb->kta', tiles, picked, preferred_element_type=jnp.floa...]
    ppermute x24 -> x0, starting transfers between devices: 64 us -> none  [the longest x12 33.8 us: from_behind(): return lax.ppermute(value, axis, pairs)]
    another operation x38 -> x0, other arithmetic: 40.9 us -> none  [the longest x18 21.6 us: on_device(): lower = jnp.linalg.cholesky(gram)]
  transfers between devices with their start and end apart: 30 -> 0, of which waited for: 7 -> 0; matrix products, arithmetic and copies ran while one was open for 4% -> 0% of each run, Pallas kernels for 0% -> 0%
where the time goes in v1:
time: 224 us
  Pallas kernels  217 us (97%)
  local copies, waits for them, and re-layouts  5.58 us (2%)
    pallas_call x1, Pallas kernels, lanczos(): pl.pallas_call(lanczos_kernel, out_shape=(jax.ShapeDtypeStruct(panel, F32...  213 us
    unnamed x17, local copies, waits for them, and re-layouts  5.58 us

profile of v1, /device:TPU:1, one launch (start us, length us, event | category | flops | bytes accessed | tf_op | source)
XLA Modules:
  0.0 223.8 jit_solution(17793304345767406503)
XLA Ops:
  0.6 0.0 copy-start.4
  1.3 0.0 copy-start
  1.3 2.2 copy-done
  3.5 0.0 copy-start.5
  3.5 0.7 copy-done.5
  4.1 0.0 copy-start.6
  4.1 0.7 copy-done.6
  4.8 0.0 copy-start.1
  4.8 0.0 copy-start.2
  4.8 0.0 copy-start.3
  4.8 3.4 %band.1.band_hbm = bf16[16,256,768]{2,1,0:T(8,128)(2,1)S(1)} custom-call(s32[1,128]{1,0:T(1,128)S(1)} %bitcast.10, s32[1,128]{1,0:T(1,128)S(1)} %bitcast.11, s32[1,1]{1,0:T(1,128)S(6)} %copy.14.count_ref, bf16[128,128,128]{2,1,0:T(8,128)(2,1)S(1)} %bitcast.6), custom_call_target="tpu_custom_call" | custom-call | tf_op jit(solution)/shard_map/band/pallas_call | solution.py:76
  8.2 0.0 copy-done.4
  8.2 0.0 copy-done.1
  8.2 0.0 copy-done.2
  8.2 0.0 copy-done.3
  8.3 213.4 %lanczos.1 = (f32[32,256]{1,0:T(8,128)S(1)}, f32[6,32,32]{2,1,0:T(8,128)S(1)}, f32[6,32,32]{2,1,0:T(8,128)S(1)}) custom-call(bf16[16,256,768]{2,1,0:T(8,128)(2,1)S(1)} %band.1.band_hbm, f32[1,256]{1,0:T(1,128)S(1)} %bitcast.9, f32[32,256]{1,0:T(8,128)S(1)} %copy-done.1, f32[32,256]{1,0:T(8,128)S(1)} %copy-done.2, f32[32,32]{1,0:T(8,128)S(1)} %copy-done.3), custom_call_target="tpu_custom_call" | custom-call | tf_op jit(solution)/shard_map/lanczos/pallas_call | solution.py:364
  221.7 0.7 copy.11
  222.4 0.7 copy.12
  223.2 0.6 copy.15
Async XLA Ops:
  0.6 7.6 %copy-start.4 = (f32[256]{0:T(256)S(1)}, f32[256]{0:T(256)}, u32[]{:S(2)}) copy-start(f32[256]{0:T(256)} %param.12) | copy-start | bytes 3076
  1.3 2.2 copy-start
  3.5 0.7 copy-start.5
  4.1 0.7 copy-start.6
  4.8 3.4 %copy-start.1 = (f32[32,256]{1,0:T(8,128)S(1)}, f32[32,256]{1,0:T(8,128)}, u32[]{:S(2)}) copy-start(f32[32,256]{1,0:T(8,128)} %prev_ref.1) | copy-start | bytes 98308
  4.8 3.4 %copy-start.2 = (f32[32,256]{1,0:T(8,128)S(1)}, f32[32,256]{1,0:T(8,128)}, u32[]{:S(2)}) copy-start(f32[32,256]{1,0:T(8,128)} %cur_ref.1) | copy-start | bytes 98308
  4.8 3.4 %copy-start.3 = (f32[32,32]{1,0:T(8,128)S(1)}, f32[32,32]{1,0:T(8,128)}, u32[]{:S(2)}) copy-start(f32[32,32]{1,0:T(8,128)} %coup_ref.1) | copy-start | bytes 12292

commit v2 on v1

v2 whole, which is shorter than its diff:
```python
import jax
import jax.numpy as jnp
from jax import lax
from jax.experimental import pallas as pl
from jax.experimental.pallas import tpu as pltpu
from jax.sharding import PartitionSpec as P

ITERS = 6
K = 32
BS = 128
WIDTH = 256
N_ROW = 16
N_COL = 16
SLOTS = 128
PLANE = 8
MESH_IDS = pl.DeviceIdType.MESH
F32 = jnp.float32
BF16 = jnp.bfloat16


def dot_nn(left, right):
    return lax.dot_general(
        left, right, (((1,), (0,)), ((), ())), precision=lax.Precision.HIGHEST, preferred_element_type=F32
    )


def dot_nt(left, right):
    return lax.dot_general(
        left, right, (((1,), (1,)), ((), ())), precision=lax.Precision.HIGHEST, preferred_element_type=F32
    )


def band_kernel(rows_ref, cols_ref, count_ref, tiles_hbm, band_ref, tiles, total, sems):
    parts = 4
    size = SLOTS // parts
    copies = [
        pltpu.make_async_copy(
            tiles_hbm.at[pl.ds(k * size, size)], tiles.at[pl.ds(k * size, size)], sems.at[k]
        )
        for k in range(parts)
    ]
    for copy in copies:
        copy.start()

    def clear(i, carry):
        total[i] = jnp.zeros(total.shape[1:], F32)
        return carry

    lax.fori_loop(0, 2 * N_COL, clear, 0)
    first_col = 2 * (lax.axis_index("row") - 1)
    count = count_ref[0, 0]

    def add(slot, carry):
        i = rows_ref[0, slot]
        j = cols_ref[0, slot] - first_col
        total[i, j] += tiles[slot].astype(F32)
        return carry

    for k in range(parts):
        copies[k].wait()
        lax.fori_loop(k * size, jnp.minimum((k + 1) * size, count), add, 0)

    def place(c, carry):
        for half in range(2):
            for j in range(6):
                band_ref[c, half * BS : (half + 1) * BS, j * BS : (j + 1) * BS] = total[
                    2 * c + half, j
                ].astype(BF16)
        return carry

    lax.fori_loop(0, N_COL, place, 0)


def build_band(tiles, rows, cols, count):
    smem = pl.BlockSpec(memory_space=pltpu.SMEM)
    return pl.pallas_call(
        band_kernel,
        out_shape=jax.ShapeDtypeStruct((N_COL, 2 * BS, 6 * BS), BF16),
        in_specs=[smem, smem, smem, pl.BlockSpec(memory_space=pl.ANY)],
        out_specs=pl.BlockSpec(memory_space=pltpu.VMEM),
        scratch_shapes=[
            pltpu.VMEM((SLOTS, BS, BS), BF16),
            pltpu.VMEM((2 * N_COL, 6, BS, BS), F32),
            pltpu.SemaphoreType.DMA((4,)),
        ],
        compiler_params=pltpu.CompilerParams(vmem_limit_bytes=40 * 2**20),
        name="band",
    )(rows, cols, count, tiles)


def factor(gram):
    groups = K // 8
    sub = lax.broadcasted_iota(jnp.int32, (8, K), 0)
    lane = lax.broadcasted_iota(jnp.int32, (8, K), 1)
    g = [gram[8 * b : 8 * b + 8] for b in range(groups)]
    e = [jnp.where(lane == sub + 8 * b, 1.0, 0.0).astype(F32) for b in range(groups)]
    step = 4
    for base in range(0, K, step):
        a = base // 8
        spread = [
            [
                jnp.broadcast_to(g[b][:, base + j : base + j + 1], (8, K)) if b >= a else None
                for b in range(groups)
            ]
            for j in range(step)
        ]
        for j in range(step):
            s = (base + j) % 8
            pivot = spread[j][a][s : s + 1]
            guess = lax.rsqrt(pivot)
            scale = guess * (1.5 - 0.5 * (pivot * guess) * guess)
            g_row = g[a][s : s + 1] * scale
            e_row = e[a][s : s + 1] * scale
            later = {jj: spread[jj][a][s : s + 1] * scale for jj in range(j + 1, step)}
            for b in range(a, groups):
                part = spread[j][b] * scale
                if b == a:
                    part = jnp.where(sub > s, part, 0.0)
                g[b] = g[b] - part * g_row
                e[b] = e[b] - part * e_row
                for jj in range(j + 1, step):
                    spread[jj][b] = spread[jj][b] - part * later[jj]
            g[a] = jnp.where(sub == s, g_row, g[a])
            e[a] = jnp.where(sub == s, e_row, e[a])
    upper = [jnp.where(lane >= sub + 8 * b, g[b], 0.0) for b in range(groups)]
    return jnp.concatenate(upper, axis=0), jnp.concatenate(e, axis=0)


def lanczos_kernel(
    band_hbm, noise_ref, prev_ref, cur_ref, coup_ref,
    out_ref, diag_ref, upper_ref,
    band, ty, coup, xband, xrows, facc, fsend, fown, frecv, zsend, zrecv, msend, mrecv, mir,
    hloc, h1, s2, h2, h3,
    band_sem, send_sems, recv_sems, sum_send, sum_recv,
):
    r = lax.axis_index("row")
    c = lax.axis_index("col")
    x, zl = r // 4, r % 4
    zh, p = c // PLANE, c % PLANE
    z = zh * 4 + zl
    m = x * 8 + z
    up = (lax.rem(r + 1, N_ROW), c)
    down = (lax.rem(r + N_ROW - 1, N_ROW), c)
    over = (r, lax.rem(c + PLANE, N_COL))

    def plane_dev(pp):
        return (r, zh * PLANE + pp)

    def sheet_dev(d):
        xx = lax.rem(x + 2 + d // 8, 4)
        zz = lax.rem(z + 4 + d % 8, 8)
        return (xx * 4 + zz % 4, (zz // 4) * PLANE + p)

    def on_plane(body):
        lax.fori_loop(1, PLANE, lambda d, carry: (body(d, lax.rem(p + d, PLANE)), carry)[1], 0)

    def on_sheet(body):
        lax.fori_loop(0, 20, lambda d, carry: (body(sheet_dev(d)), carry)[1], 0)
        lax.fori_loop(21, 32, lambda d, carry: (body(sheet_dev(d)), carry)[1], 0)

    def put(src, dst, send, recv, dev):
        pltpu.make_async_remote_copy(
            src_ref=src, dst_ref=dst, send_sem=send, recv_sem=recv, device_id=dev, device_id_type=MESH_IDS
        ).start()

    def take(ref, sem):
        pltpu.make_async_copy(ref, ref, sem).wait()

    load = pltpu.make_async_copy(band_hbm, band, band_sem)
    load.start()

    barrier = pltpu.get_barrier_semaphore()

    def greet(dev):
        pl.semaphore_signal(barrier, inc=1, device_id=dev, device_id_type=MESH_IDS)

    on_sheet(greet)
    on_plane(lambda d, pp: greet(plane_dev(pp)))
    ty[...] = jnp.zeros_like(ty)
    ty[K : 2 * K, :WIDTH] = cur_ref[...]
    ty[2 * K :, :WIDTH] = prev_ref[...]
    coup[...] = coup_ref[...]
    pl.semaphore_wait(barrier, 7 + 31)


    def spread(n, par):
        own = xband.at[par, 1, pl.ds(0, n)]
        put(own, xband.at[par, 0, pl.ds(0, n)], send_sems.at[0], recv_sems.at[par, 0], up)
        put(own, xband.at[par, 2, pl.ds(0, n)], send_sems.at[0], recv_sems.at[par, 0], down)
        place = xrows.at[par, zh, p, pl.ds(0, n)]
        put(own, place, send_sems.at[1], recv_sems.at[par, 1], over)
        on_plane(lambda d, pp: put(own, place, send_sems.at[2], recv_sems.at[par, 2], plane_dev(pp)))
        xrows[par, zh, p, :n] = xband[par, 1, :n]

    def own_forward(n, par):
        def body(k, carry):
            for u in range(4):
                facc[4 * k + u, :n] = lax.dot_general(
                    xband[par, 1, :n], band[4 * k + u, :, WIDTH : 2 * WIDTH], (((1,), (1,)), ((), ())),
                    preferred_element_type=F32,
                )
            return carry

        lax.fori_loop(0, 4, body, 0)

    def pass_on(n, par):
        take(xband.at[par, pl.ds(0, 2), pl.ds(0, n)], recv_sems.at[par, 0])
        take(zrecv.at[par, pl.ds(0, n)], recv_sems.at[par, 1])
        other = xrows.at[par, 1 - zh, p, pl.ds(0, n)]
        on_plane(lambda d, pp: put(other, other, send_sems.at[3], recv_sems.at[par, 3], plane_dev(pp)))

    def forward(n, par, half):
        hi = 1 - zh if half == 0 else zh

        def product(pp):
            acc = facc[hi * PLANE + pp, :n]
            for g in (0, 2):
                acc = acc + lax.dot_general(
                    xband[par, g, :n], band[hi * PLANE + pp, :, g * WIDTH : (g + 1) * WIDTH],
                    (((1,), (1,)), ((), ())), preferred_element_type=F32,
                )
            return acc

        def send(d):
            put(
                fsend.at[half, d - 1, pl.ds(0, n)], frecv.at[par, half, d - 1, pl.ds(0, n)],
                send_sems.at[4 + half], recv_sems.at[par, 4 + half], plane_dev(lax.rem(p + d, PLANE)),
            )

        def body(k, carry):
            d = 2 * k + 1
            first = product(lax.rem(p + d, PLANE))
            second = product(lax.rem(p + d + 1, PLANE))
            fsend[half, d - 1, :n] = first.astype(BF16)
            fsend[half, d, :n] = second.astype(BF16)
            send(d)
            send(d + 1)
            return carry

        lax.fori_loop(0, 3, body, 0)
        first = product(lax.rem(p + 7, PLANE))
        second = product(p)
        fsend[half, 6, :n] = first.astype(BF16)
        fown[half, :n] = second
        send(7)

    def seven(n):
        return xrows.at[0, 0, pl.ds(0, 7), pl.ds(0, n)]

    def mirror(n, par, hi, first):
        def body(k, carry):
            acc = None
            for u in range(4):
                pp = 4 * k + u
                term = jnp.dot(
                    xrows[par, hi, pp, :n], band[hi * PLANE + pp], preferred_element_type=F32
                )
                acc = term if acc is None else acc + term
            if first:
                mir[:n] = jnp.where(k == 0, acc, mir[:n] + acc)
            else:
                mir[:n] += acc
            return carry

        lax.fori_loop(0, 2, body, 0)

    def mirror_near(n, par):
        take(seven(n), recv_sems.at[par, 2])
        mirror(n, par, zh, True)

    def mirror_far(n, par):
        take(seven(n), recv_sems.at[par, 3])
        mirror(n, par, 1 - zh, False)
        msend[0, :n] = mir[:n, :WIDTH].astype(BF16)
        msend[1, :n] = mir[:n, 2 * WIDTH :].astype(BF16)
        for g, dev in ((0, down), (1, up)):
            put(
                msend.at[g, pl.ds(0, n)], mrecv.at[par, g, pl.ds(0, n)],
                send_sems.at[6], recv_sems.at[par, 6], dev,
            )

    def total(n, par, half):
        take(frecv.at[par, half, :, pl.ds(0, n)], recv_sems.at[par, 4 + half])
        acc = fown[half, :n]
        for d in range(7):
            acc = acc + frecv[par, half, d, :n].astype(F32)
        return acc

    def send_over(n, par):
        zsend[:n] = total(n, par, 0).astype(BF16)
        put(
            zsend.at[pl.ds(0, n)], zrecv.at[par, pl.ds(0, n)], send_sems.at[7], recv_sems.at[par, 7], over
        )

    def gather_image(n, par, vectors):
        acc = total(n, par, 1) + mir[:n, WIDTH : 2 * WIDTH] + noise_ref[...] * vectors
        take(mrecv.at[par, :, pl.ds(0, n)], recv_sems.at[par, 6])
        acc = acc + mrecv[par, 0, :n].astype(F32) + mrecv[par, 1, :n].astype(F32)
        take(zrecv.at[par, pl.ds(0, n)], recv_sems.at[par, 7])
        return acc + zrecv[par, :n].astype(F32)

    def all_left(n):
        one = zsend.at[pl.ds(0, n)]
        take(msend.at[:, pl.ds(0, n)], send_sems.at[0])
        take(one, send_sems.at[1])
        take(seven(n), send_sems.at[2])
        take(seven(n), send_sems.at[3])
        take(seven(n), send_sems.at[4])
        take(seven(n), send_sems.at[5])
        take(msend.at[:, pl.ds(0, n)], send_sems.at[6])
        take(one, send_sems.at[7])

    xband[1, 1, :K] = cur_ref[...].astype(BF16)
    xband[1, 1, K:] = prev_ref[...].astype(BF16)
    spread(2 * K, 1)
    load.wait()
    own_forward(2 * K, 1)
    pass_on(2 * K, 1)
    forward(2 * K, 1, 0)
    forward(2 * K, 1, 1)
    mirror_near(2 * K, 1)
    mirror_far(2 * K, 1)
    send_over(2 * K, 1)
    images = gather_image(2 * K, 1, ty[K:, :WIDTH])
    ty[K:, WIDTH:] = images
    xband[0, 1, :K] = images[:K].astype(BF16)
    all_left(2 * K)

    def iteration(it, carry):
        par = lax.rem(it, 2)
        more = it < ITERS - 1

        @pl.when(more)
        def _():
            spread(K, par)

        ty[:K, :WIDTH] = xband[par, 1, :K].astype(F32)
        y = ty[:, :WIDTH]
        gram = dot_nt(y, jnp.concatenate([y, y[2 * K :]], axis=0))
        lane = lax.broadcasted_iota(jnp.int32, (K, 4 * K), 1)
        top = jnp.where(lane < 3 * K, gram[0:K], gram[2 * K : 3 * K])
        hloc[0:4] = top.reshape(4, 8, 4 * K)
        hloc[4:8] = gram[K : 2 * K].reshape(4, 8, 4 * K)
        on_plane(lambda d, pp: put(hloc.at[pp], h1.at[p], sum_send.at[0], sum_recv.at[0], plane_dev(pp)))
        h1[p] = hloc[p]

        @pl.when(more)
        def _():
            own_forward(K, par)

        take(h1.at[pl.ds(0, 7)], sum_recv.at[0])
        piece = jnp.sum(h1[...], axis=0)
        s2[...] = piece
        h2[par, m] = piece
        on_sheet(lambda dev: put(s2, h2.at[par, m], sum_send.at[1], sum_recv.at[1 + par], dev))

        @pl.when(more)
        def _():
            pass_on(K, par)
            forward(K, par, 0)
            forward(K, par, 1)
            mirror_near(K, par)
            mirror_far(K, par)
            send_over(K, par)

        take(h2.at[par, pl.ds(0, 31)], sum_recv.at[1 + par])
        h3[p] = jnp.sum(h2[par], axis=0)
        on_plane(lambda d, pp: put(h3.at[p], h3.at[p], sum_send.at[2], sum_recv.at[3], plane_dev(pp)))

        @pl.when(more)
        def _():
            ty[:K, WIDTH:] = gather_image(K, par, ty[:K, :WIDTH])

        take(h1.at[pl.ds(0, 7)], sum_recv.at[3])
        h = h3[...].reshape(8 * PLANE, 4 * K) * (1.0 / (N_ROW * N_COL * WIDTH))

        im_im, im_q, im_p, p_p = (h[0:K, k * K : (k + 1) * K] for k in range(4))
        q_im, q_q, q_p = (h[K : 2 * K, k * K : (k + 1) * K] for k in range(3))
        b = coup[...]
        diag_t = im_q - dot_nt(b, q_p)
        cp = b + (im_p - dot_nn(b, p_p) - dot_nn(diag_t, q_p))
        third = ty[:K] - dot_nn(cp, ty[2 * K :]) - dot_nn(diag_t, ty[K : 2 * K])
        t_im = im_im - dot_nn(diag_t, q_im) - dot_nt(cp, im_p)
        t_q = im_q - dot_nn(diag_t, q_q) - dot_nt(cp, q_p)
        t_p = im_p - dot_nn(diag_t, q_p) - dot_nn(cp, p_p)
        upper, inverse = factor(t_im - dot_nt(t_q, diag_t) - dot_nt(t_p, cp))
        following = dot_nn(inverse, third)
        diag_ref[it] = diag_t
        upper_ref[it] = upper
        coup[...] = upper
        ty[2 * K :] = ty[K : 2 * K]
        ty[K : 2 * K] = following
        xband[1 - par, 1, :K] = following[:, WIDTH:].astype(BF16)

        @pl.when(more)
        def _():
            all_left(K)

        take(h1.at[pl.ds(0, 7)], sum_send.at[0])
        take(h2.at[par, pl.ds(0, 31)], sum_send.at[1])
        take(h1.at[pl.ds(0, 7)], sum_send.at[2])
        return carry

    lax.fori_loop(0, ITERS, iteration, 0)
    out_ref[...] = ty[K : 2 * K, :WIDTH]


def lanczos(band, noise, previous, current, coupling):
    vmem = pl.BlockSpec(memory_space=pltpu.VMEM)
    panel = (K, WIDTH)
    two = (2 * K, WIDTH)
    piece = (8, 4 * K)
    return pl.pallas_call(
        lanczos_kernel,
        out_shape=(
            jax.ShapeDtypeStruct(panel, F32),
            jax.ShapeDtypeStruct((ITERS, K, K), F32),
            jax.ShapeDtypeStruct((ITERS, K, K), F32),
        ),
        in_specs=[pl.BlockSpec(memory_space=pl.ANY), vmem, vmem, vmem, vmem],
        out_specs=(vmem, vmem, vmem),
        scratch_shapes=[
            pltpu.VMEM((N_COL, 2 * BS, 6 * BS), BF16),
            pltpu.VMEM((3 * K, 2 * WIDTH), F32),
            pltpu.VMEM((K, K), F32),
            pltpu.VMEM((2, 3) + two, BF16),
            pltpu.VMEM((2, 2, PLANE) + two, BF16),
            pltpu.VMEM((N_COL,) + two, F32),
            pltpu.VMEM((2, 7) + two, BF16),
            pltpu.VMEM((2,) + two, F32),
            pltpu.VMEM((2, 2, 7) + two, BF16),
            pltpu.VMEM(two, BF16),
            pltpu.VMEM((2,) + two, BF16),
            pltpu.VMEM((2,) + two, BF16),
            pltpu.VMEM((2, 2) + two, BF16),
            pltpu.VMEM((2 * K, 3 * WIDTH), F32),
            pltpu.VMEM((8,) + piece, F32),
            pltpu.VMEM((8,) + piece, F32),
            pltpu.VMEM(piece, F32),
            pltpu.VMEM((2, 32) + piece, F32),
            pltpu.VMEM((8,) + piece, F32),
            pltpu.SemaphoreType.DMA,
            pltpu.SemaphoreType.DMA((8,)),
            pltpu.SemaphoreType.DMA((2, 8)),
            pltpu.SemaphoreType.DMA((3,)),
            pltpu.SemaphoreType.DMA((4,)),
        ],
        compiler_params=pltpu.CompilerParams(
            collective_id=0, has_side_effects=True, vmem_limit_bytes=40 * 2**20
        ),
        name="lanczos",
    )(band, noise, previous, current, coupling)


def on_device(
    kernel_tiles, tile_rows, tile_cols, tile_counts, noise, prev_block, current_block, prev_coupling
):
    band = build_band(kernel_tiles[0, 0], tile_rows[0], tile_cols[0], tile_counts)
    following, diag_t, upper = lanczos(band, noise[None, :], prev_block, current_block, prev_coupling)
    return (following, jnp.swapaxes(diag_t, 1, 2), jnp.swapaxes(upper, 1, 2))


def solution(mesh):
    in_specs = (
        P("row", "col", None, None, None),
        P("row", "col", None),
        P("row", "col", None),
        P("row", "col"),
        P(("row", "col")),
        P(None, ("row", "col")),
        P(None, ("row", "col")),
        P(),
    )
    out_specs = (P(None, ("row", "col")), P(), P())
    return jax.shard_map(
        on_device, mesh=mesh, in_specs=in_specs, out_specs=out_specs, check_vma=False
    )
```

time: 224 us -> 154 us (0.69)
  Pallas kernels: 217 us -> 146 us
    pallas_call x1, Pallas kernels: 213 us -> 143 us  [lanczos(): pl.pallas_call(lanczos_kernel, out_shape=(jax.ShapeDtypeStruct(panel, F32...]
where the time goes in v2:
time: 154 us; the launch traced here: 153 us
  Pallas kernels  146 us (95%)
  local copies, waits for them, and re-layouts  5.58 us (4%)
    pallas_call x1, Pallas kernels, lanczos(): pl.pallas_call(lanczos_kernel, out_shape=(jax.ShapeDtypeStruct(panel, F32...  143 us
    unnamed x17, local copies, waits for them, and re-layouts  5.58 us
    pallas_call x1, Pallas kernels, build_band(): pl.pallas_call(band_kernel, out_shape=jax.ShapeDtypeStruct((N_COL, 2 * BS...  3.66 us

profile of v2, /device:TPU:1, one launch (start us, length us, event | category | flops | bytes accessed | tf_op | source)
XLA Modules:
  0.0 153.4 jit_solution(9375054305027316248)
XLA Ops:
  0.6 0.0 copy-start.4
  1.3 0.0 copy-start
  1.3 2.2 %copy-done = bf16[1,1,128,128,128]{4,3,2,1,0:T(8,128)(2,1)S(1)} copy-done((bf16[1,1,128,128,128]{4,3,2,1,0:T(8,128)(2,1)S(1)}, bf16[1,1,128,128,128]{4,3,2,1,0:T(8,128)(2,1)}, u32[]{:S(2)}) %copy-start) | copy-done | bytes 4194328
  3.5 0.0 copy-start.5
  3.5 0.7 copy-done.5
  4.1 0.0 copy-start.6
  4.1 0.7 copy-done.6
  4.8 0.0 copy-start.1
  4.8 0.0 copy-start.2
  4.8 0.0 copy-start.3
  4.8 3.7 %band.1.band_hbm = bf16[16,256,768]{2,1,0:T(8,128)(2,1)S(1)} custom-call(s32[1,128]{1,0:T(1,128)S(1)} %bitcast.10, s32[1,128]{1,0:T(1,128)S(1)} %bitcast.11, s32[1,1]{1,0:T(1,128)S(6)} %copy.14.count_ref, bf16[128,128,128]{2,1,0:T(8,128)(2,1)S(1)} %bitcast.6), custom_call_target="tpu_custom_call" | custom-call | tf_op jit(solution)/shard_map/band/pallas_call | solution.py:76
  8.5 0.0 copy-done.4
  8.5 0.0 copy-done.1
  8.5 0.0 copy-done.2
  8.5 0.0 copy-done.3
  8.5 142.8 %lanczos.1 = (f32[32,256]{1,0:T(8,128)S(1)}, f32[6,32,32]{2,1,0:T(8,128)S(1)}, f32[6,32,32]{2,1,0:T(8,128)S(1)}) custom-call(bf16[16,256,768]{2,1,0:T(8,128)(2,1)S(1)} %band.1.band_hbm, f32[1,256]{1,0:T(1,128)S(1)} %bitcast.9, f32[32,256]{1,0:T(8,128)S(1)} %copy-done.1, f32[32,256]{1,0:T(8,128)S(1)} %copy-done.2, f32[32,32]{1,0:T(8,128)S(1)} %copy-done.3), custom_call_target="tpu_custom_call" | custom-call | tf_op jit(solution)/shard_map/lanczos/pallas_call | solution.py:413
  151.4 0.7 copy.11
  152.1 0.7 copy.12
  152.8 0.6 copy.15
Async XLA Ops:
  0.6 7.8 %copy-start.4 = (f32[256]{0:T(256)S(1)}, f32[256]{0:T(256)}, u32[]{:S(2)}) copy-start(f32[256]{0:T(256)} %param.12) | copy-start | bytes 3076
  1.3 2.2 %copy-start = (bf16[1,1,128,128,128]{4,3,2,1,0:T(8,128)(2,1)S(1)}, bf16[1,1,128,128,128]{4,3,2,1,0:T(8,128)(2,1)}, u32[]{:S(2)}) copy-start(bf16[1,1,128,128,128]{4,3,2,1,0:T(8,128)(2,1)} %param.8) | copy-start | bytes 12582916
  3.5 0.7 copy-start.5
  4.1 0.7 copy-start.6
  4.8 3.7 %copy-start.1 = (f32[32,256]{1,0:T(8,128)S(1)}, f32[32,256]{1,0:T(8,128)}, u32[]{:S(2)}) copy-start(f32[32,256]{1,0:T(8,128)} %prev_ref.1) | copy-start | bytes 98308
  4.8 3.7 %copy-start.2 = (f32[32,256]{1,0:T(8,128)S(1)}, f32[32,256]{1,0:T(8,128)}, u32[]{:S(2)}) copy-start(f32[32,256]{1,0:T(8,128)} %cur_ref.1) | copy-start | bytes 98308
  4.8 3.7 %copy-start.3 = (f32[32,32]{1,0:T(8,128)S(1)}, f32[32,32]{1,0:T(8,128)}, u32[]{:S(2)}) copy-start(f32[32,32]{1,0:T(8,128)} %coup_ref.1) | copy-start | bytes 12292

commit v3 on v2

--- a/solution.py
+++ b/solution.py
@@ -127,11 +127,11 @@
 
 
 def lanczos_kernel(
-    band_hbm, noise_ref, prev_ref, cur_ref, coup_ref,
+    band, noise_ref, prev_ref, cur_ref, coup_ref,
     out_ref, diag_ref, upper_ref,
-    band, ty, coup, xband, xrows, facc, fsend, fown, frecv, zsend, zrecv, msend, mrecv, mir,
+    ty, known, xband, xrows, facc, fsend, fown, frecv, zsend, zrecv, msend, mrecv, mir,
     hloc, h1, s2, h2, h3,
-    band_sem, send_sems, recv_sems, sum_send, sum_recv,
+    send_sems, recv_sems, sum_send, sum_recv,
 ):
     r = lax.axis_index("row")
     c = lax.axis_index("col")
@@ -166,9 +166,6 @@
     def take(ref, sem):
         pltpu.make_async_copy(ref, ref, sem).wait()
 
-    load = pltpu.make_async_copy(band_hbm, band, band_sem)
-    load.start()
-
     barrier = pltpu.get_barrier_semaphore()
 
     def greet(dev):
@@ -179,7 +176,7 @@
     ty[...] = jnp.zeros_like(ty)
     ty[K : 2 * K, :WIDTH] = cur_ref[...]
     ty[2 * K :, :WIDTH] = prev_ref[...]
-    coup[...] = coup_ref[...]
+    known[0] = coup_ref[...]
     pl.semaphore_wait(barrier, 7 + 31)
 
 
@@ -310,49 +307,78 @@
         take(msend.at[:, pl.ds(0, n)], send_sems.at[6])
         take(one, send_sems.at[7])
 
+
+    def sum_first(part):
+        for k in range(PLANE):
+            hloc[k] = part[4 * k : 4 * k + 4]
+        on_plane(lambda d, pp: put(hloc.at[pp], h1.at[p], sum_send.at[0], sum_recv.at[0], plane_dev(pp)))
+        h1[p] = hloc[p]
+
+    def sum_second(par):
+        take(h1.at[pl.ds(0, 7)], sum_recv.at[0])
+        piece = jnp.sum(h1[...], axis=0)
+        s2[...] = piece
+        h2[par, m] = piece
+        on_sheet(lambda dev: put(s2, h2.at[par, m], sum_send.at[1], sum_recv.at[1 + par], dev))
+
+    def sum_third(par):
+        take(h2.at[par, pl.ds(0, 31)], sum_recv.at[1 + par])
+        h3[p] = jnp.sum(h2[par], axis=0)
+        on_plane(lambda d, pp: put(h3.at[p], h3.at[p], sum_send.at[2], sum_recv.at[3], plane_dev(pp)))
+
+    def sum_result():
+        take(h1.at[pl.ds(0, 7)], sum_recv.at[3])
+        h = jnp.concatenate([h3[k] for k in range(PLANE)], axis=0)
+        h = h * (1.0 / (N_ROW * N_COL * WIDTH))
+        return [h[:, k * K : (k + 1) * K] for k in range(3)]
+
+    def sum_left(par):
+        take(h1.at[pl.ds(0, 7)], sum_send.at[0])
+        take(h2.at[par, pl.ds(0, 31)], sum_send.at[1])
+        take(h1.at[pl.ds(0, 7)], sum_send.at[2])
+
+    lane = lax.broadcasted_iota(jnp.int32, (K, 4 * K), 1)
+
     xband[1, 1, :K] = cur_ref[...].astype(BF16)
     xband[1, 1, K:] = prev_ref[...].astype(BF16)
     spread(2 * K, 1)
-    load.wait()
+    q_and_p = ty[K:, :WIDTH]
+    both = dot_nt(q_and_p, jnp.concatenate([q_and_p, ty[2 * K :, :WIDTH], ty[2 * K :, :WIDTH]], axis=0))
+    sum_first(jnp.where(lane < 2 * K, both[:K], both[K:]))
     own_forward(2 * K, 1)
+    sum_second(1)
     pass_on(2 * K, 1)
     forward(2 * K, 1, 0)
     forward(2 * K, 1, 1)
     mirror_near(2 * K, 1)
     mirror_far(2 * K, 1)
     send_over(2 * K, 1)
+    sum_third(1)
     images = gather_image(2 * K, 1, ty[K:, :WIDTH])
     ty[K:, WIDTH:] = images
     xband[0, 1, :K] = images[:K].astype(BF16)
     all_left(2 * K)
+    spread(K, 0)
+    for k, value in enumerate(sum_result()):
+        known[1 + k] = value
+    sum_left(1)
 
     def iteration(it, carry):
         par = lax.rem(it, 2)
         more = it < ITERS - 1
 
-        @pl.when(more)
-        def _():
-            spread(K, par)
-
         ty[:K, :WIDTH] = xband[par, 1, :K].astype(F32)
         y = ty[:, :WIDTH]
-        gram = dot_nt(y, jnp.concatenate([y, y[2 * K :]], axis=0))
-        lane = lax.broadcasted_iota(jnp.int32, (K, 4 * K), 1)
-        top = jnp.where(lane < 3 * K, gram[0:K], gram[2 * K : 3 * K])
-        hloc[0:4] = top.reshape(4, 8, 4 * K)
-        hloc[4:8] = gram[K : 2 * K].reshape(4, 8, 4 * K)
-        on_plane(lambda d, pp: put(hloc.at[pp], h1.at[p], sum_send.at[0], sum_recv.at[0], plane_dev(pp)))
-        h1[p] = hloc[p]
+        sum_first(dot_nt(y[:K], jnp.concatenate([y, y[2 * K :]], axis=0)))
+        b, q_q, q_p, p_p = (known[k] for k in range(4))
+        b_qp = dot_nt(b, q_p)
+        b_pp = b - dot_nn(b, p_p)
 
         @pl.when(more)
         def _():
             own_forward(K, par)
 
-        take(h1.at[pl.ds(0, 7)], sum_recv.at[0])
-        piece = jnp.sum(h1[...], axis=0)
-        s2[...] = piece
-        h2[par, m] = piece
-        on_sheet(lambda dev: put(s2, h2.at[par, m], sum_send.at[1], sum_recv.at[1 + par], dev))
+        sum_second(par)
 
         @pl.when(more)
         def _():
@@ -363,42 +389,42 @@
             mirror_far(K, par)
             send_over(K, par)
 
-        take(h2.at[par, pl.ds(0, 31)], sum_recv.at[1 + par])
-        h3[p] = jnp.sum(h2[par], axis=0)
-        on_plane(lambda d, pp: put(h3.at[p], h3.at[p], sum_send.at[2], sum_recv.at[3], plane_dev(pp)))
+        sum_third(par)
+        im_im, im_q, im_p = sum_result()
+        diag_t = im_q - b_qp
+        cp = im_p + b_pp - dot_nn(diag_t, q_p)
+        t_im = im_im - dot_nt(diag_t, im_q) - dot_nt(cp, im_p)
+        t_q = im_q - dot_nn(diag_t, q_q) - dot_nt(cp, q_p)
+        t_p = im_p - dot_nn(diag_t, q_p) - dot_nn(cp, p_p)
+        gram = t_im - dot_nt(t_q, diag_t) - dot_nt(t_p, cp)
+        rest = dot_nn(cp, ty[2 * K :]) + dot_nn(diag_t, ty[K : 2 * K])
+        upper, inverse = factor(gram)
 
         @pl.when(more)
         def _():
             ty[:K, WIDTH:] = gather_image(K, par, ty[:K, :WIDTH])
 
-        take(h1.at[pl.ds(0, 7)], sum_recv.at[3])
-        h = h3[...].reshape(8 * PLANE, 4 * K) * (1.0 / (N_ROW * N_COL * WIDTH))
-
-        im_im, im_q, im_p, p_p = (h[0:K, k * K : (k + 1) * K] for k in range(4))
-        q_im, q_q, q_p = (h[K : 2 * K, k * K : (k + 1) * K] for k in range(3))
-        b = coup[...]
-        diag_t = im_q - dot_nt(b, q_p)
-        cp = b + (im_p - dot_nn(b, p_p) - dot_nn(diag_t, q_p))
-        third = ty[:K] - dot_nn(cp, ty[2 * K :]) - dot_nn(diag_t, ty[K : 2 * K])
-        t_im = im_im - dot_nn(diag_t, q_im) - dot_nt(cp, im_p)
-        t_q = im_q - dot_nn(diag_t, q_q) - dot_nt(cp, q_p)
-        t_p = im_p - dot_nn(diag_t, q_p) - dot_nn(cp, p_p)
-        upper, inverse = factor(t_im - dot_nt(t_q, diag_t) - dot_nt(t_p, cp))
-        following = dot_nn(inverse, third)
-        diag_ref[it] = diag_t
-        upper_ref[it] = upper
-        coup[...] = upper
-        ty[2 * K :] = ty[K : 2 * K]
-        ty[K : 2 * K] = following
+        following = dot_nn(inverse, ty[:K] - rest)
         xband[1 - par, 1, :K] = following[:, WIDTH:].astype(BF16)
 
         @pl.when(more)
         def _():
             all_left(K)
 
-        take(h1.at[pl.ds(0, 7)], sum_send.at[0])
-        take(h2.at[par, pl.ds(0, 31)], sum_send.at[1])
-        take(h1.at[pl.ds(0, 7)], sum_send.at[2])
+        sum_left(par)
+
+        @pl.when(it < ITERS - 2)
+        def _():
+            spread(K, 1 - par)
+
+        ty[2 * K :] = ty[K : 2 * K]
+        ty[K : 2 * K] = following
+        diag_ref[it] = diag_t
+        upper_ref[it] = upper
+        known[0] = upper
+        known[1] = dot_nt(dot_nn(inverse, gram), inverse)
+        known[2] = dot_nn(inverse, t_q)
+        known[3] = q_q
         return carry
 
     lax.fori_loop(0, ITERS, iteration, 0)
@@ -409,7 +435,7 @@
     vmem = pl.BlockSpec(memory_space=pltpu.VMEM)
     panel = (K, WIDTH)
     two = (2 * K, WIDTH)
-    piece = (8, 4 * K)
+    piece = (4, 4 * K)
     return pl.pallas_call(
         lanczos_kernel,
         out_shape=(
@@ -417,12 +443,11 @@
             jax.ShapeDtypeStruct((ITERS, K, K), F32),
             jax.ShapeDtypeStruct((ITERS, K, K), F32),
         ),
-        in_specs=[pl.BlockSpec(memory_space=pl.ANY), vmem, vmem, vmem, vmem],
+        in_specs=[vmem, vmem, vmem, vmem, vmem],
         out_specs=(vmem, vmem, vmem),
         scratch_shapes=[
-            pltpu.VMEM((N_COL, 2 * BS, 6 * BS), BF16),
             pltpu.VMEM((3 * K, 2 * WIDTH), F32),
-            pltpu.VMEM((K, K), F32),
+            pltpu.VMEM((4, K, K), F32),
             pltpu.VMEM((2, 3) + two, BF16),
             pltpu.VMEM((2, 2, PLANE) + two, BF16),
             pltpu.VMEM((N_COL,) + two, F32),
@@ -439,7 +464,6 @@
             pltpu.VMEM(piece, F32),
             pltpu.VMEM((2, 32) + piece, F32),
             pltpu.VMEM((8,) + piece, F32),
-            pltpu.SemaphoreType.DMA,
             pltpu.SemaphoreType.DMA((8,)),
             pltpu.SemaphoreType.DMA((2, 8)),
             pltpu.SemaphoreType.DMA((3,)),

time: 154 us -> 143 us (0.929)
  Pallas kernels: 146 us -> 136 us
    pallas_call x1, Pallas kernels: 143 us -> 132 us  [lanczos(): pl.pallas_call(lanczos_kernel, out_shape=(jax.ShapeDtypeStruct(panel, F32...]
where the time goes in v3:
time: 143 us
  Pallas kernels  136 us (95%)
  local copies, waits for them, and re-layouts  5.58 us (4%)
    pallas_call x1, Pallas kernels, lanczos(): pl.pallas_call(lanczos_kernel, out_shape=(jax.ShapeDtypeStruct(panel, F32...  132 us
    unnamed x17, local copies, waits for them, and re-layouts  5.58 us
    pallas_call x1, Pallas kernels, build_band(): pl.pallas_call(band_kernel, out_shape=jax.ShapeDtypeStruct((N_COL, 2 * BS...  3.8 us

profile of v3, /device:TPU:1, one launch (start us, length us, event | category | flops | bytes accessed | tf_op | source)
XLA Modules:
  0.0 143.0 jit_solution(3519260980394533793)
XLA Ops:
  0.6 0.0 copy-start.4
  1.3 0.0 copy-start
  1.3 2.2 %copy-done = bf16[1,1,128,128,128]{4,3,2,1,0:T(8,128)(2,1)S(1)} copy-done((bf16[1,1,128,128,128]{4,3,2,1,0:T(8,128)(2,1)S(1)}, bf16[1,1,128,128,128]{4,3,2,1,0:T(8,128)(2,1)}, u32[]{:S(2)}) %copy-start) | copy-done | bytes 4194328
  3.5 0.0 copy-start.5
  3.5 0.7 copy-done.5
  4.1 0.0 copy-start.6
  4.1 0.7 copy-done.6
  4.8 0.0 copy-start.1
  4.8 0.0 copy-start.2
  4.8 0.0 copy-start.3
  4.8 3.8 %band.1 = bf16[16,256,768]{2,1,0:T(8,128)(2,1)S(1)} custom-call(s32[1,128]{1,0:T(1,128)S(1)} %bitcast.10, s32[1,128]{1,0:T(1,128)S(1)} %bitcast.11, s32[1,1]{1,0:T(1,128)S(6)} %copy.14.count_ref, bf16[128,128,128]{2,1,0:T(8,128)(2,1)S(1)} %bitcast.6), custom_call_target="tpu_custom_call" | custom-call | tf_op jit(solution)/shard_map/band/pallas_call | solution.py:76
  8.6 0.0 copy-done.4
  8.6 0.0 copy-done.1
  8.6 0.0 copy-done.2
  8.6 0.0 copy-done.3
  8.7 132.3 %lanczos.1 = (f32[32,256]{1,0:T(8,128)S(1)}, f32[6,32,32]{2,1,0:T(8,128)S(1)}, f32[6,32,32]{2,1,0:T(8,128)S(1)}) custom-call(bf16[16,256,768]{2,1,0:T(8,128)(2,1)S(1)} %band.1, f32[1,256]{1,0:T(1,128)S(1)} %bitcast.9, f32[32,256]{1,0:T(8,128)S(1)} %copy-done.1, f32[32,256]{1,0:T(8,128)S(1)} %copy-done.2, f32[32,32]{1,0:T(8,128)S(1)} %copy-done.3), custom_call_target="tpu_custom_call" | custom-call | tf_op jit(solution)/shard_map/lanczos/pallas_call | solution.py:439
  141.0 0.7 copy.11
  141.7 0.7 copy.12
  142.4 0.6 copy.15
Async XLA Ops:
  0.6 8.0 %copy-start.4 = (f32[256]{0:T(256)S(1)}, f32[256]{0:T(256)}, u32[]{:S(2)}) copy-start(f32[256]{0:T(256)} %param.12) | copy-start | bytes 3076
  1.3 2.2 %copy-start = (bf16[1,1,128,128,128]{4,3,2,1,0:T(8,128)(2,1)S(1)}, bf16[1,1,128,128,128]{4,3,2,1,0:T(8,128)(2,1)}, u32[]{:S(2)}) copy-start(bf16[1,1,128,128,128]{4,3,2,1,0:T(8,128)(2,1)} %param.8) | copy-start | bytes 12582916
  3.5 0.7 copy-start.5
  4.1 0.7 copy-start.6
  4.8 3.8 %copy-start.1 = (f32[32,256]{1,0:T(8,128)S(1)}, f32[32,256]{1,0:T(8,128)}, u32[]{:S(2)}) copy-start(f32[32,256]{1,0:T(8,128)} %prev_ref.1) | copy-start | bytes 98308
  4.8 3.8 %copy-start.2 = (f32[32,256]{1,0:T(8,128)S(1)}, f32[32,256]{1,0:T(8,128)}, u32[]{:S(2)}) copy-start(f32[32,256]{1,0:T(8,128)} %cur_ref.1) | copy-start | bytes 98308
  4.8 3.8 %copy-start.3 = (f32[32,32]{1,0:T(8,128)S(1)}, f32[32,32]{1,0:T(8,128)}, u32[]{:S(2)}) copy-start(f32[32,32]{1,0:T(8,128)} %coup_ref.1) | copy-start | bytes 12292

commit v4 on v3

--- a/solution.py
+++ b/solution.py
@@ -30,18 +30,7 @@
     )
 
 
-def band_kernel(rows_ref, cols_ref, count_ref, tiles_hbm, band_ref, tiles, total, sems):
-    parts = 4
-    size = SLOTS // parts
-    copies = [
-        pltpu.make_async_copy(
-            tiles_hbm.at[pl.ds(k * size, size)], tiles.at[pl.ds(k * size, size)], sems.at[k]
-        )
-        for k in range(parts)
-    ]
-    for copy in copies:
-        copy.start()
-
+def band_kernel(rows_ref, cols_ref, count_ref, tiles, band_ref, total):
     def clear(i, carry):
         total[i] = jnp.zeros(total.shape[1:], F32)
         return carry
@@ -56,9 +45,7 @@
         total[i, j] += tiles[slot].astype(F32)
         return carry
 
-    for k in range(parts):
-        copies[k].wait()
-        lax.fori_loop(k * size, jnp.minimum((k + 1) * size, count), add, 0)
+    lax.fori_loop(0, count, add, 0)
 
     def place(c, carry):
         for half in range(2):
@@ -76,12 +63,10 @@
     return pl.pallas_call(
         band_kernel,
         out_shape=jax.ShapeDtypeStruct((N_COL, 2 * BS, 6 * BS), BF16),
-        in_specs=[smem, smem, smem, pl.BlockSpec(memory_space=pl.ANY)],
+        in_specs=[smem, smem, smem, pl.BlockSpec(memory_space=pltpu.VMEM)],
         out_specs=pl.BlockSpec(memory_space=pltpu.VMEM),
         scratch_shapes=[
-            pltpu.VMEM((SLOTS, BS, BS), BF16),
             pltpu.VMEM((2 * N_COL, 6, BS, BS), F32),
-            pltpu.SemaphoreType.DMA((4,)),
         ],
         compiler_params=pltpu.CompilerParams(vmem_limit_bytes=40 * 2**20),
         name="band",
@@ -129,7 +114,7 @@
 def lanczos_kernel(
     band, noise_ref, prev_ref, cur_ref, coup_ref,
     out_ref, diag_ref, upper_ref,
-    ty, known, xband, xrows, facc, fsend, fown, frecv, zsend, zrecv, msend, mrecv, mir,
+    ty, known, held, split, xband, xrows, facc, fsend, fown, frecv, zsend, zrecv, msend, mrecv, mir,
     hloc, h1, s2, h2, h3,
     send_sems, recv_sems, sum_send, sum_recv,
 ):
@@ -224,22 +209,14 @@
                 send_sems.at[4 + half], recv_sems.at[par, 4 + half], plane_dev(lax.rem(p + d, PLANE)),
             )
 
-        def body(k, carry):
-            d = 2 * k + 1
-            first = product(lax.rem(p + d, PLANE))
-            second = product(lax.rem(p + d + 1, PLANE))
-            fsend[half, d - 1, :n] = first.astype(BF16)
-            fsend[half, d, :n] = second.astype(BF16)
-            send(d)
-            send(d + 1)
-            return carry
-
-        lax.fori_loop(0, 3, body, 0)
-        first = product(lax.rem(p + 7, PLANE))
-        second = product(p)
-        fsend[half, 6, :n] = first.astype(BF16)
-        fown[half, :n] = second
-        send(7)
+        for first in (1, 5):
+            parts = [product(lax.rem(p + first + u, PLANE)) for u in range(4)]
+            for u in range(4):
+                if first + u < PLANE:
+                    fsend[half, first + u - 1, :n] = parts[u].astype(BF16)
+                    send(first + u)
+                else:
+                    fown[half, :n] = parts[u]
 
     def seven(n):
         return xrows.at[0, 0, pl.ds(0, 7), pl.ds(0, n)]
@@ -289,8 +266,10 @@
             zsend.at[pl.ds(0, n)], zrecv.at[par, pl.ds(0, n)], send_sems.at[7], recv_sems.at[par, 7], over
         )
 
-    def gather_image(n, par, vectors):
-        acc = total(n, par, 1) + mir[:n, WIDTH : 2 * WIDTH] + noise_ref[...] * vectors
+    def image_here(n, par, vectors):
+        return total(n, par, 1) + mir[:n, WIDTH : 2 * WIDTH] + noise_ref[...] * vectors
+
+    def image_whole(n, par, acc):
         take(mrecv.at[par, :, pl.ds(0, n)], recv_sems.at[par, 6])
         acc = acc + mrecv[par, 0, :n].astype(F32) + mrecv[par, 1, :n].astype(F32)
         take(zrecv.at[par, pl.ds(0, n)], recv_sems.at[par, 7])
@@ -338,6 +317,16 @@
         take(h1.at[pl.ds(0, 7)], sum_send.at[2])
 
     lane = lax.broadcasted_iota(jnp.int32, (K, 4 * K), 1)
+
+    def split_in_three(value, start):
+        for k in range(3):
+            part = value.astype(BF16)
+            split[k, start : start + K] = part
+            value = value - part.astype(F32)
+
+    split[...] = jnp.zeros_like(split)
+    split_in_three(cur_ref[...], 0)
+    split_in_three(prev_ref[...], K)
 
     xband[1, 1, :K] = cur_ref[...].astype(BF16)
     xband[1, 1, K:] = prev_ref[...].astype(BF16)
@@ -354,11 +343,11 @@
     mirror_far(2 * K, 1)
     send_over(2 * K, 1)
     sum_third(1)
-    images = gather_image(2 * K, 1, ty[K:, :WIDTH])
+    images = image_whole(2 * K, 1, image_here(2 * K, 1, ty[K:, :WIDTH]))
     ty[K:, WIDTH:] = images
     xband[0, 1, :K] = images[:K].astype(BF16)
+    ty[:K, :WIDTH] = xband[0, 1, :K].astype(F32)
     all_left(2 * K)
-    spread(K, 0)
     for k, value in enumerate(sum_result()):
         known[1 + k] = value
     sum_left(1)
@@ -367,12 +356,31 @@
         par = lax.rem(it, 2)
         more = it < ITERS - 1
 
-        ty[:K, :WIDTH] = xband[par, 1, :K].astype(F32)
-        y = ty[:, :WIDTH]
-        sum_first(dot_nt(y[:K], jnp.concatenate([y, y[2 * K :]], axis=0)))
+        image = xband[par, 1, :K]
+        split[0, 2 * K : 3 * K] = image
+        terms = [
+            lax.dot_general(
+                image, split[k], (((1,), (1,)), ((), ())), preferred_element_type=F32
+            )
+            for k in range(3)
+        ]
+        sum_first(terms[0] + terms[1] + terms[2])
+
+        @pl.when(more)
+        def _():
+            spread(K, par)
+
+        @pl.when(it > 0)
+        def _():
+            known[3] = known[1]
+            known[1] = dot_nt(dot_nn(held[0], held[1]), held[0])
+            known[2] = dot_nn(held[0], held[2])
+
         b, q_q, q_p, p_p = (known[k] for k in range(4))
         b_qp = dot_nt(b, q_p)
         b_pp = b - dot_nn(b, p_p)
+        q_rest = q_q - dot_nt(q_p, q_p)
+        p_rest = q_p - dot_nn(q_p, p_p)
 
         @pl.when(more)
         def _():
@@ -386,45 +394,50 @@
             forward(K, par, 0)
             forward(K, par, 1)
             mirror_near(K, par)
+
+        sum_third(par)
+
+        @pl.when(more)
+        def _():
             mirror_far(K, par)
             send_over(K, par)
-
-        sum_third(par)
-        im_im, im_q, im_p = sum_result()
+            ty[:K, WIDTH:] = image_here(K, par, ty[:K, :WIDTH])
+
+        im_q, im_p, im_im = sum_result()
         diag_t = im_q - b_qp
-        cp = im_p + b_pp - dot_nn(diag_t, q_p)
-        t_im = im_im - dot_nt(diag_t, im_q) - dot_nt(cp, im_p)
-        t_q = im_q - dot_nn(diag_t, q_q) - dot_nt(cp, q_p)
-        t_p = im_p - dot_nn(diag_t, q_p) - dot_nn(cp, p_p)
-        gram = t_im - dot_nt(t_q, diag_t) - dot_nt(t_p, cp)
+        back = im_p + b_pp
+        cp = back - dot_nn(diag_t, q_p)
+        t_q = im_q - dot_nt(back, q_p) - dot_nn(diag_t, q_rest)
+        t_p = im_p - dot_nn(back, p_p) - dot_nn(diag_t, p_rest)
+        gram = im_im - dot_nt(diag_t, im_q) - dot_nt(cp, im_p) - dot_nt(t_q, diag_t) - dot_nt(t_p, cp)
         rest = dot_nn(cp, ty[2 * K :]) + dot_nn(diag_t, ty[K : 2 * K])
         upper, inverse = factor(gram)
 
         @pl.when(more)
         def _():
-            ty[:K, WIDTH:] = gather_image(K, par, ty[:K, :WIDTH])
+            ty[:K, WIDTH:] = image_whole(K, par, ty[:K, WIDTH:])
 
         following = dot_nn(inverse, ty[:K] - rest)
-        xband[1 - par, 1, :K] = following[:, WIDTH:].astype(BF16)
-
-        @pl.when(more)
-        def _():
-            all_left(K)
-
-        sum_left(par)
-
-        @pl.when(it < ITERS - 2)
-        def _():
-            spread(K, 1 - par)
-
+        rounded = following[:, WIDTH:].astype(BF16)
+        xband[1 - par, 1, :K] = rounded
+        for k in range(3):
+            split[k, K : 2 * K] = split[k, :K]
+        split_in_three(following[:, :WIDTH], 0)
         ty[2 * K :] = ty[K : 2 * K]
         ty[K : 2 * K] = following
+        ty[:K, :WIDTH] = rounded.astype(F32)
         diag_ref[it] = diag_t
         upper_ref[it] = upper
         known[0] = upper
-        known[1] = dot_nt(dot_nn(inverse, gram), inverse)
-        known[2] = dot_nn(inverse, t_q)
-        known[3] = q_q
+        held[0] = inverse
+        held[1] = gram
+        held[2] = t_q
+
+        @pl.when(more)
+        def _():
+            all_left(K)
+
+        sum_left(par)
         return carry
 
     lax.fori_loop(0, ITERS, iteration, 0)
@@ -448,6 +461,8 @@
         scratch_shapes=[
             pltpu.VMEM((3 * K, 2 * WIDTH), F32),
             pltpu.VMEM((4, K, K), F32),
+            pltpu.VMEM((3, K, K), F32),
+            pltpu.VMEM((3, 4 * K, WIDTH), BF16),
             pltpu.VMEM((2, 3) + two, BF16),
             pltpu.VMEM((2, 2, PLANE) + two, BF16),
             pltpu.VMEM((N_COL,) + two, F32),

time: 143 us -> 139 us (0.972)
  Pallas kernels: 136 us -> 132 us
    pallas_call x1, Pallas kernels: 132 us -> 128 us  [lanczos(): pl.pallas_call(lanczos_kernel, out_shape=(jax.ShapeDtypeStruct(panel, F32...]
where the time goes in v4:
time: 139 us
  Pallas kernels  132 us (95%)
  local copies, waits for them, and re-layouts  5.58 us (4%)
    pallas_call x1, Pallas kernels, lanczos(): pl.pallas_call(lanczos_kernel, out_shape=(jax.ShapeDtypeStruct(panel, F32...  128 us
    unnamed x17, local copies, waits for them, and re-layouts  5.58 us
    pallas_call x1, Pallas kernels, build_band(): pl.pallas_call(band_kernel, out_shape=jax.ShapeDtypeStruct((N_COL, 2 * BS...  3.28 us

profile of v4, /device:TPU:1, one launch (start us, length us, event | category | flops | bytes accessed | tf_op | source)
XLA Modules:
  0.0 138.5 jit_solution(2840378399344571146)
XLA Ops:
  0.6 0.0 copy-start.4
  1.3 0.0 copy-start
  1.3 2.2 %copy-done = bf16[1,1,128,128,128]{4,3,2,1,0:T(8,128)(2,1)S(1)} copy-done((bf16[1,1,128,128,128]{4,3,2,1,0:T(8,128)(2,1)S(1)}, bf16[1,1,128,128,128]{4,3,2,1,0:T(8,128)(2,1)}, u32[]{:S(2)}) %copy-start) | copy-done | bytes 4194328
  3.5 0.0 copy-start.5
  3.5 0.7 copy-done.5
  4.1 0.0 copy-start.6
  4.1 0.7 copy-done.6
  4.8 0.0 copy-start.1
  4.8 0.0 copy-start.2
  4.8 0.0 copy-start.3
  4.8 3.3 %band.1 = bf16[16,256,768]{2,1,0:T(8,128)(2,1)S(1)} custom-call(s32[1,128]{1,0:T(1,128)S(1)} %bitcast.10, s32[1,128]{1,0:T(1,128)S(1)} %bitcast.11, s32[1,1]{1,0:T(1,128)S(6)} %copy.14.count_ref, bf16[128,128,128]{2,1,0:T(8,128)(2,1)S(1)} %bitcast.6), custom_call_target="tpu_custom_call" | custom-call | tf_op jit(solution)/shard_map/band/pallas_call | solution.py:63
  8.1 0.0 copy-done.4
  8.1 0.0 copy-done.1
  8.1 0.0 copy-done.2
  8.1 0.0 copy-done.3
  8.1 128.3 %lanczos.1 = (f32[32,256]{1,0:T(8,128)S(1)}, f32[6,32,32]{2,1,0:T(8,128)S(1)}, f32[6,32,32]{2,1,0:T(8,128)S(1)}) custom-call(bf16[16,256,768]{2,1,0:T(8,128)(2,1)S(1)} %band.1, f32[1,256]{1,0:T(1,128)S(1)} %bitcast.9, f32[32,256]{1,0:T(8,128)S(1)} %copy-done.1, f32[32,256]{1,0:T(8,128)S(1)} %copy-done.2, f32[32,32]{1,0:T(8,128)S(1)} %copy-done.3), custom_call_target="tpu_custom_call" | custom-call | tf_op jit(solution)/shard_map/lanczos/pallas_call | solution.py:452
  136.4 0.7 copy.11
  137.2 0.7 copy.12
  137.9 0.6 copy.15
Async XLA Ops:
  0.6 7.5 %copy-start.4 = (f32[256]{0:T(256)S(1)}, f32[256]{0:T(256)}, u32[]{:S(2)}) copy-start(f32[256]{0:T(256)} %param.12) | copy-start | bytes 3076
  1.3 2.2 %copy-start = (bf16[1,1,128,128,128]{4,3,2,1,0:T(8,128)(2,1)S(1)}, bf16[1,1,128,128,128]{4,3,2,1,0:T(8,128)(2,1)}, u32[]{:S(2)}) copy-start(bf16[1,1,128,128,128]{4,3,2,1,0:T(8,128)(2,1)} %param.8) | copy-start | bytes 12582916
  3.5 0.7 copy-start.5
  4.1 0.7 copy-start.6
  4.8 3.3 %copy-start.1 = (f32[32,256]{1,0:T(8,128)S(1)}, f32[32,256]{1,0:T(8,128)}, u32[]{:S(2)}) copy-start(f32[32,256]{1,0:T(8,128)} %prev_ref.1) | copy-start | bytes 98308
  4.8 3.3 %copy-start.2 = (f32[32,256]{1,0:T(8,128)S(1)}, f32[32,256]{1,0:T(8,128)}, u32[]{:S(2)}) copy-start(f32[32,256]{1,0:T(8,128)} %cur_ref.1) | copy-start | bytes 98308
  4.8 3.3 %copy-start.3 = (f32[32,32]{1,0:T(8,128)S(1)}, f32[32,32]{1,0:T(8,128)}, u32[]{:S(2)}) copy-start(f32[32,32]{1,0:T(8,128)} %coup_ref.1) | copy-start | bytes 12292

commit v5 on v4

--- a/solution.py
+++ b/solution.py
@@ -137,7 +137,8 @@
         return (xx * 4 + zz % 4, (zz // 4) * PLANE + p)
 
     def on_plane(body):
-        lax.fori_loop(1, PLANE, lambda d, carry: (body(d, lax.rem(p + d, PLANE)), carry)[1], 0)
+        lax.fori_loop(3, PLANE, lambda d, carry: (body(d, lax.rem(p + d, PLANE)), carry)[1], 0)
+        lax.fori_loop(1, 3, lambda d, carry: (body(d, lax.rem(p + d, PLANE)), carry)[1], 0)
 
     def on_sheet(body):
         lax.fori_loop(0, 20, lambda d, carry: (body(sheet_dev(d)), carry)[1], 0)
@@ -314,7 +315,6 @@
     def sum_left(par):
         take(h1.at[pl.ds(0, 7)], sum_send.at[0])
         take(h2.at[par, pl.ds(0, 31)], sum_send.at[1])
-        take(h1.at[pl.ds(0, 7)], sum_send.at[2])
 
     lane = lax.broadcasted_iota(jnp.int32, (K, 4 * K), 1)
 
@@ -351,6 +351,7 @@
     for k, value in enumerate(sum_result()):
         known[1 + k] = value
     sum_left(1)
+    take(h1.at[pl.ds(0, 7)], sum_send.at[2])
 
     def iteration(it, carry):
         par = lax.rem(it, 2)
@@ -402,7 +403,9 @@
             mirror_far(K, par)
             send_over(K, par)
             ty[:K, WIDTH:] = image_here(K, par, ty[:K, :WIDTH])
-
+            all_left(K)
+
+        sum_left(par)
         im_q, im_p, im_im = sum_result()
         diag_t = im_q - b_qp
         back = im_p + b_pp
@@ -432,12 +435,7 @@
         held[0] = inverse
         held[1] = gram
         held[2] = t_q
-
-        @pl.when(more)
-        def _():
-            all_left(K)
-
-        sum_left(par)
+        take(h1.at[pl.ds(0, 7)], sum_send.at[2])
         return carry
 
     lax.fori_loop(0, ITERS, iteration, 0)

time: 139 us -> 138 us (level)
  Pallas kernels: 132 us -> 130 us
    pallas_call x1, Pallas kernels: 128 us -> 127 us  [lanczos(): pl.pallas_call(lanczos_kernel, out_shape=(jax.ShapeDtypeStruct(panel, F32...]
where the time goes in v5:
time: 138 us; the launch traced here: 137 us
  Pallas kernels  130 us (94%)
  local copies, waits for them, and re-layouts  5.58 us (4%)
    pallas_call x1, Pallas kernels, lanczos(): pl.pallas_call(lanczos_kernel, out_shape=(jax.ShapeDtypeStruct(panel, F32...  127 us
    unnamed x17, local copies, waits for them, and re-layouts  5.58 us
    pallas_call x1, Pallas kernels, build_band(): pl.pallas_call(band_kernel, out_shape=jax.ShapeDtypeStruct((N_COL, 2 * BS...  3.38 us

profile of v5, /device:TPU:1, one launch (start us, length us, event | category | flops | bytes accessed | tf_op | source)
XLA Modules:
  0.0 137.1 jit_solution(14730606132176601364)
XLA Ops:
  0.6 0.0 copy-start.4
  1.3 0.0 copy-start
  1.3 2.2 %copy-done = bf16[1,1,128,128,128]{4,3,2,1,0:T(8,128)(2,1)S(1)} copy-done((bf16[1,1,128,128,128]{4,3,2,1,0:T(8,128)(2,1)S(1)}, bf16[1,1,128,128,128]{4,3,2,1,0:T(8,128)(2,1)}, u32[]{:S(2)}) %copy-start) | copy-done | bytes 4194328
  3.5 0.0 copy-start.5
  3.5 0.7 copy-done.5
  4.1 0.0 copy-start.6
  4.1 0.7 copy-done.6
  4.8 0.0 copy-start.1
  4.8 0.0 copy-start.2
  4.8 0.0 copy-start.3
  4.8 3.4 %band.1 = bf16[16,256,768]{2,1,0:T(8,128)(2,1)S(1)} custom-call(s32[1,128]{1,0:T(1,128)S(1)} %bitcast.10, s32[1,128]{1,0:T(1,128)S(1)} %bitcast.11, s32[1,1]{1,0:T(1,128)S(6)} %copy.14.count_ref, bf16[128,128,128]{2,1,0:T(8,128)(2,1)S(1)} %bitcast.6), custom_call_target="tpu_custom_call" | custom-call | tf_op jit(solution)/shard_map/band/pallas_call | solution.py:63
  8.2 0.0 copy-done.4
  8.2 0.0 copy-done.1
  8.2 0.0 copy-done.2
  8.2 0.0 copy-done.3
  8.2 126.8 %lanczos.1 = (f32[32,256]{1,0:T(8,128)S(1)}, f32[6,32,32]{2,1,0:T(8,128)S(1)}, f32[6,32,32]{2,1,0:T(8,128)S(1)}) custom-call(bf16[16,256,768]{2,1,0:T(8,128)(2,1)S(1)} %band.1, f32[1,256]{1,0:T(1,128)S(1)} %bitcast.9, f32[32,256]{1,0:T(8,128)S(1)} %copy-done.1, f32[32,256]{1,0:T(8,128)S(1)} %copy-done.2, f32[32,32]{1,0:T(8,128)S(1)} %copy-done.3), custom_call_target="tpu_custom_call" | custom-call | tf_op jit(solution)/shard_map/lanczos/pallas_call | solution.py:450
  135.1 0.7 copy.11
  135.8 0.7 copy.12
  136.5 0.6 copy.15
Async XLA Ops:
  0.6 7.6 %copy-start.4 = (f32[256]{0:T(256)S(1)}, f32[256]{0:T(256)}, u32[]{:S(2)}) copy-start(f32[256]{0:T(256)} %param.12) | copy-start | bytes 3076
  1.3 2.2 %copy-start = (bf16[1,1,128,128,128]{4,3,2,1,0:T(8,128)(2,1)S(1)}, bf16[1,1,128,128,128]{4,3,2,1,0:T(8,128)(2,1)}, u32[]{:S(2)}) copy-start(bf16[1,1,128,128,128]{4,3,2,1,0:T(8,128)(2,1)} %param.8) | copy-start | bytes 12582916
  3.5 0.7 copy-start.5
  4.1 0.7 copy-start.6
  4.8 3.4 %copy-start.1 = (f32[32,256]{1,0:T(8,128)S(1)}, f32[32,256]{1,0:T(8,128)}, u32[]{:S(2)}) copy-start(f32[32,256]{1,0:T(8,128)} %prev_ref.1) | copy-start | bytes 98308
  4.8 3.4 %copy-start.2 = (f32[32,256]{1,0:T(8,128)S(1)}, f32[32,256]{1,0:T(8,128)}, u32[]{:S(2)}) copy-start(f32[32,256]{1,0:T(8,128)} %cur_ref.1) | copy-start | bytes 98308
  4.8 3.4 %copy-start.3 = (f32[32,32]{1,0:T(8,128)S(1)}, f32[32,32]{1,0:T(8,128)}, u32[]{:S(2)}) copy-start(f32[32,32]{1,0:T(8,128)} %coup_ref.1) | copy-start | bytes 12292

commit v6 on v5

--- a/solution.py
+++ b/solution.py
@@ -163,7 +163,6 @@
     ty[K : 2 * K, :WIDTH] = cur_ref[...]
     ty[2 * K :, :WIDTH] = prev_ref[...]
     known[0] = coup_ref[...]
-    pl.semaphore_wait(barrier, 7 + 31)
 
 
     def spread(n, par):
@@ -330,9 +329,10 @@
 
     xband[1, 1, :K] = cur_ref[...].astype(BF16)
     xband[1, 1, K:] = prev_ref[...].astype(BF16)
-    spread(2 * K, 1)
     q_and_p = ty[K:, :WIDTH]
     both = dot_nt(q_and_p, jnp.concatenate([q_and_p, ty[2 * K :, :WIDTH], ty[2 * K :, :WIDTH]], axis=0))
+    pl.semaphore_wait(barrier, 7 + 31)
+    spread(2 * K, 1)
     sum_first(jnp.where(lane < 2 * K, both[:K], both[K:]))
     own_forward(2 * K, 1)
     sum_second(1)

time: 138 us -> 138 us (level)
    pallas_call x1, Pallas kernels: 127 us -> 128 us  [lanczos(): pl.pallas_call(lanczos_kernel, out_shape=(jax.ShapeDtypeStruct(panel, F32...]
where the time goes in v6:
time: 138 us
  Pallas kernels  131 us (95%)
  local copies, waits for them, and re-layouts  5.58 us (4%)
    pallas_call x1, Pallas kernels, lanczos(): pl.pallas_call(lanczos_kernel, out_shape=(jax.ShapeDtypeStruct(panel, F32...  128 us
    unnamed x17, local copies, waits for them, and re-layouts  5.58 us
    pallas_call x1, Pallas kernels, build_band(): pl.pallas_call(band_kernel, out_shape=jax.ShapeDtypeStruct((N_COL, 2 * BS...  2.88 us

profile of v6, /device:TPU:1, one launch (start us, length us, event | category | flops | bytes accessed | tf_op | source)
XLA Modules:
  0.0 138.3 jit_solution(14274647002693912377)
XLA Ops:
  0.6 0.0 copy-start.4
  1.3 0.0 copy-start
  1.3 2.2 %copy-done = bf16[1,1,128,128,128]{4,3,2,1,0:T(8,128)(2,1)S(1)} copy-done((bf16[1,1,128,128,128]{4,3,2,1,0:T(8,128)(2,1)S(1)}, bf16[1,1,128,128,128]{4,3,2,1,0:T(8,128)(2,1)}, u32[]{:S(2)}) %copy-start) | copy-done | bytes 4194328
  3.5 0.0 copy-start.5
  3.5 0.7 copy-done.5
  4.1 0.0 copy-start.6
  4.1 0.7 copy-done.6
  4.8 0.0 copy-start.1
  4.8 0.0 copy-start.2
  4.8 0.0 copy-start.3
  4.8 2.9 %band.1 = bf16[16,256,768]{2,1,0:T(8,128)(2,1)S(1)} custom-call(s32[1,128]{1,0:T(1,128)S(1)} %bitcast.10, s32[1,128]{1,0:T(1,128)S(1)} %bitcast.11, s32[1,1]{1,0:T(1,128)S(6)} %copy.14.count_ref, bf16[128,128,128]{2,1,0:T(8,128)(2,1)S(1)} %bitcast.6), custom_call_target="tpu_custom_call" | custom-call | tf_op jit(solution)/shard_map/band/pallas_call | solution.py:63
  7.7 0.0 copy-done.4
  7.7 0.0 copy-done.1
  7.7 0.0 copy-done.2
  7.7 0.0 copy-done.3
  7.7 128.4 %lanczos.1 = (f32[32,256]{1,0:T(8,128)S(1)}, f32[6,32,32]{2,1,0:T(8,128)S(1)}, f32[6,32,32]{2,1,0:T(8,128)S(1)}) custom-call(bf16[16,256,768]{2,1,0:T(8,128)(2,1)S(1)} %band.1, f32[1,256]{1,0:T(1,128)S(1)} %bitcast.9, f32[32,256]{1,0:T(8,128)S(1)} %copy-done.1, f32[32,256]{1,0:T(8,128)S(1)} %copy-done.2, f32[32,32]{1,0:T(8,128)S(1)} %copy-done.3), custom_call_target="tpu_custom_call" | custom-call | tf_op jit(solution)/shard_map/lanczos/pallas_call | solution.py:450
  136.2 0.7 copy.11
  136.9 0.7 copy.12
  137.7 0.6 copy.15
Async XLA Ops:
  0.6 7.1 %copy-start.4 = (f32[256]{0:T(256)S(1)}, f32[256]{0:T(256)}, u32[]{:S(2)}) copy-start(f32[256]{0:T(256)} %param.12) | copy-start | bytes 3076
  1.3 2.2 %copy-start = (bf16[1,1,128,128,128]{4,3,2,1,0:T(8,128)(2,1)S(1)}, bf16[1,1,128,128,128]{4,3,2,1,0:T(8,128)(2,1)}, u32[]{:S(2)}) copy-start(bf16[1,1,128,128,128]{4,3,2,1,0:T(8,128)(2,1)} %param.8) | copy-start | bytes 12582916
  3.5 0.7 copy-start.5
  4.1 0.7 copy-start.6
  4.8 2.9 %copy-start.1 = (f32[32,256]{1,0:T(8,128)S(1)}, f32[32,256]{1,0:T(8,128)}, u32[]{:S(2)}) copy-start(f32[32,256]{1,0:T(8,128)} %prev_ref.1) | copy-start | bytes 98308
  4.8 2.9 %copy-start.2 = (f32[32,256]{1,0:T(8,128)S(1)}, f32[32,256]{1,0:T(8,128)}, u32[]{:S(2)}) copy-start(f32[32,256]{1,0:T(8,128)} %cur_ref.1) | copy-start | bytes 98308
  4.8 2.9 %copy-start.3 = (f32[32,32]{1,0:T(8,128)S(1)}, f32[32,32]{1,0:T(8,128)}, u32[]{:S(2)}) copy-start(f32[32,32]{1,0:T(8,128)} %coup_ref.1) | copy-start | bytes 12292
